TPU v7x, 128 devices: a whole 4x4x4 slice. The times are simulated.
128 devices in a mesh: seq: 32 (over x, y, core), sub: 4 (over z).
Axes of the slice: x: 4, y: 4, z: 4, core: 2. Of those that a mesh axis runs over, the one named last changes fastest.
Arguments:
- queries: bfloat16 [32768, 512], P(('seq', 'sub')), may hold values from -128 to 128
- keys: bfloat16 [32768, 128], P(('seq', 'sub')), may hold values from -8 to 8
- values: bfloat16 [32768, 128], P(('seq', 'sub')), may hold values from -6 to 6
- dout: bfloat16 [32768, 512], P(('seq', 'sub')), may hold values from -6 to 6
- doc_lengths: int32 [32], replicated, may hold values from 1 to 8192, 32768 in all
Outputs:
- attended: bfloat16 [32768, 512], P(('seq', 'sub'))
- query_grad: bfloat16 [32768, 512], P(('seq', 'sub'))
- key_grad: bfloat16 [32768, 128], P(('seq', 'sub'))
- value_grad: bfloat16 [32768, 128], P(('seq', 'sub'))
Inputs may be any that keep to these rules, and one draw needn't show every extreme that they name: `doc_lengths`: each document has 1 to 8192 tokens, one exactly 8192, and together they fill the batch.
All inputs are finite; a program needn't handle non-finite values.
Results may differ from a plain program's by a relative error of at most 0.04.
Values may be sent and summed in bfloat16 or wider, within the bound.
No kernel may reach another device: no remote copies, remote signals or barrier semaphores. Data moves between devices by JAX's collectives and lax.ppermute only.
A program may use at most 64 MiB of HBM per device.

v0:
```python
import functools
import math

import jax
import jax.numpy as jnp
from jax import lax
from jax.experimental import pallas as pl
from jax.experimental.pallas import tpu as pltpu
from jax.sharding import PartitionSpec as P

BIG_NEG = -1e30
LOG2E = 1.4426950408889634
HALF = 4
WINDOW = 2 * HALF + 2
LIST = 6 + WINDOW


def nt(a, b):
    return lax.dot_general(a, b, (((1,), (1,)), ((), ())), preferred_element_type=jnp.float32)


def nn(a, b):
    return lax.dot_general(a, b, (((1,), (0,)), ((), ())), preferred_element_type=jnp.float32)


def table_kernel(blk, subs, ids_ref, len_ref, near_ref, far_ref, start_ref):
    chip, core, sub, mate, far = (ids_ref[i] for i in range(5))
    q0 = [((2 * chip + core) * subs + side) * blk for side in (sub, mate)]
    qpos = [q + lax.broadcasted_iota(jnp.int32, (1, blk), 1) for q in q0]
    zero = jnp.int32(0)
    begin, first, last = zero, [zero] * 2, [zero] * 2
    found = [jnp.zeros((1, blk), jnp.int32)] * 2
    for d in range(len_ref.shape[0]):
        for r in range(2):
            first[r] = jnp.where(begin <= q0[r], begin, first[r])
            last[r] = jnp.where(begin <= q0[r] + blk - 1, begin, last[r])
            found[r] = jnp.where(begin <= qpos[r], begin, found[r])
        begin = begin + len_ref[d]
    for r in range(2):
        start_ref[r] = found[r]
    for info_ref, share in ((near_ref, sub), (far_ref, far)):
        count2, count1 = zero, zero
        for j in range(WINDOW):
            if j == 2 * HALF:
                info_ref[2] = count2
                info_ref[3] = count1
            owner = core if j < HALF or j == 2 * HALF else 1 - core
            jj = j % HALF
            back = 0 if j >= 2 * HALF else 1 + 2 * owner if jj < 2 else 2 + 2 * owner
            parity = owner if j >= 2 * HALF or jj % 2 == 0 else 1 - owner
            kstart = ((2 * (chip - back) + parity) * subs + share) * blk
            kend = kstart + blk - 1
            active = [(kend >= first[r]) & (kstart <= q0[r] + blk - 1) for r in range(2)]
            whole = [(kstart >= last[r]) & (kend <= q0[r]) for r in range(2)]
            clear = active[0] & whole[0] & active[1] & whole[1]
            mixed = (active[0] | active[1]) & jnp.logical_not(clear)
            info_ref[6 + j] = kstart
            info_ref[LIST + count2] = j
            count2 = count2 + clear.astype(jnp.int32)
            info_ref[LIST + WINDOW + count1] = j
            count1 = count1 + mixed.astype(jnp.int32)
        info_ref[0] = count2
        info_ref[1] = count1
        info_ref[4] = q0[0]
        info_ref[5] = q0[1]


def tables(ids, doc_lengths, blk, subs):
    info = jax.ShapeDtypeStruct((LIST + 2 * WINDOW,), jnp.int32)
    return pl.pallas_call(
        functools.partial(table_kernel, blk, subs),
        out_shape=(info, info, jax.ShapeDtypeStruct((2, 1, blk), jnp.int32)),
        in_specs=[sm(), sm()],
        out_specs=(sm(), sm(), vm()),
        name="tile_tables",
    )(ids, doc_lengths)


def fill(window_ref, part_refs, pieces, blk):
    at = 0
    for part, begin, count in pieces:
        for i in range(count):
            for kind in range(2):
                window_ref[kind, at] = part_refs[part][kind, (begin + i) * blk:(begin + i + 1) * blk, :]
            at += 1


def fill_heads(dest_ref, sources, heads, hd):
    for r, source in enumerate(sources):
        for h in range(heads):
            dest_ref[r * heads + h] = source[:, h * hd:(h + 1) * hd]


def fill_scaled(dest_ref, sources, heads, hd, scale):
    for r, source in enumerate(sources):
        for h in range(heads):
            whole = source[:, h * hd:(h + 1) * hd].astype(jnp.float32) * scale
            high = whole.astype(jnp.bfloat16)
            dest_ref[r * heads + h, :, :hd] = high
            dest_ref[r * heads + h, :, hd:] = (whole - high.astype(jnp.float32)).astype(jnp.bfloat16)


def over_tiles(info_ref, start_ref, bias_ref, blk, span, tile, pairs):
    begin2 = info_ref[2] if span == "own" else 0
    begin1 = info_ref[3] if span == "own" else 0
    end2 = info_ref[2] if span == "half" else info_ref[0]
    end1 = info_ref[3] if span == "half" else info_ref[1]
    base = 2 * HALF if span == "own" else 0

    def two(i, _):
        at = LIST + begin2 + 2 * i
        pairs(info_ref[at] - base, info_ref[at + 1] - base)
        return 0

    def clear(i, _):
        tile(info_ref[LIST + i] - base, None)
        return 0

    def mixed(i, _):
        j = info_ref[LIST + WINDOW + i]
        kpos = info_ref[6 + j] + lax.broadcasted_iota(jnp.int32, (blk, blk), 0)
        for r in range(2):
            qpos = info_ref[4 + r] + lax.broadcasted_iota(jnp.int32, (1, blk), 1)
            bias_ref[r] = jnp.where((kpos <= qpos) & (kpos >= start_ref[r]), 0.0, BIG_NEG)
        tile(j - base, bias_ref)
        return 0

    half = 0
    if span != "own":
        half = lax.shift_right_logical(end2 - begin2, 1)
        lax.fori_loop(0, half, two, 0)
    lax.fori_loop(begin2 + 2 * half, end2, clear, 0)
    lax.fori_loop(begin1, end1, mixed, 0)


def forward_kernel(heads, hd, share, pieces, info_ref, start_ref, q0_ref, q1_ref, *rest):
    blk = q0_ref.shape[0]
    parts = 1 + max(piece[0] for piece in pieces)
    part_refs, rest = rest[:parts], rest[parts:]
    scale = LOG2E / math.sqrt(hd)
    if share == 0:
        m_ref, l_ref, a_ref, qs_ref, window_ref, bias_ref = rest
        m_ref[...] = jnp.full(m_ref.shape, BIG_NEG, jnp.float32)
        l_ref[...] = jnp.zeros(l_ref.shape, jnp.float32)
        a_ref[...] = jnp.zeros(a_ref.shape, jnp.float32)
    else:
        m_in, l_in, a_in, d0_ref, d1_ref, stat_ref, mine_ref, theirs_ref = rest[:8]
        qs_ref, window_ref, bias_ref, m_ref, l_ref, a_ref = rest[8:]
        m_ref[...] = m_in[...]
        l_ref[...] = l_in[...]
        a_ref[...] = a_in[...]
    fill(window_ref, part_refs, pieces, blk)
    fill_scaled(qs_ref, (q0_ref, q1_ref), heads, hd, scale)

    def update(kb, vb, masks):
        xs = range(2 * heads)
        vt = jnp.concatenate([vb.T, jnp.ones((16, vb.shape[0]), jnp.bfloat16)], axis=0)
        k2 = jnp.concatenate([kb, kb], axis=1)
        old = [(m_ref[x], l_ref[x], a_ref[x]) for x in xs]
        found = [nt(k2, qs_ref[x]) for x in xs]
        if masks is not None:
            found = [s + masks[x // heads] for x, s in zip(xs, found)]
        new = []
        for s, (m_old, l_old, a_old) in zip(found, old):
            m_new = jnp.maximum(m_old, jnp.max(s, axis=0, keepdims=True))
            p = jnp.exp2(s - m_new)
            f = jnp.exp2(m_old - m_new)
            both = nn(vt, p.astype(jnp.bfloat16))
            new.append((m_new, l_old * f + both[hd:hd + 1], a_old * f + both[:hd]))
        for x, (m_new, total, acc) in zip(xs, new):
            m_ref[x] = m_new
            l_ref[x] = total
            a_ref[x] = acc

    def tile(j, masks):
        update(window_ref[0, j], window_ref[1, j], masks)

    def pairs(j1, j2):
        kb, vb = [jnp.concatenate([window_ref[i, j1], window_ref[i, j2]], axis=0) for i in range(2)]
        update(kb, vb, None)

    over_tiles(info_ref, start_ref, bias_ref, blk, "all", tile, pairs)
    if share == 1:
        for r, d_ref in enumerate((d0_ref, d1_ref)):
            for h in range(heads):
                x = r * heads + h
                dt = d_ref[:, h * hd:(h + 1) * hd].astype(jnp.float32).T
                stat_ref[x, 0:1] = m_ref[x]
                stat_ref[x, 1:2] = l_ref[x]
                stat_ref[x, 2:3] = jnp.sum(dt * a_ref[x], axis=0, keepdims=True)
        mine_ref[...] = a_ref[:heads]
        theirs_ref[...] = a_ref[heads:].astype(jnp.bfloat16)


def vm():
    return pl.BlockSpec(memory_space=pltpu.VMEM)


def sm():
    return pl.BlockSpec(memory_space=pltpu.SMEM)


def params():
    return pltpu.CompilerParams(vmem_limit_bytes=24 << 20)


def forward(info, starts, q0, q1, parts, pieces, share, state=(), douts=()):
    blk, width = q0.shape
    hd = parts[0].shape[2]
    heads = width // hd
    n = 2 * heads
    f32 = jnp.float32
    row = jax.ShapeDtypeStruct((n, 1, blk), f32)
    work = [pltpu.VMEM((n, blk, 2 * hd), q0.dtype), pltpu.VMEM((2, WINDOW, blk, hd), q0.dtype),
            pltpu.VMEM((2, blk, blk), f32)]
    if share == 0:
        shapes = (row, row, jax.ShapeDtypeStruct((n, hd, blk), f32))
    else:
        shapes = (jax.ShapeDtypeStruct((n, 3, blk), f32), jax.ShapeDtypeStruct((heads, hd, blk), f32),
                  jax.ShapeDtypeStruct((heads, hd, blk), jnp.bfloat16))
        work += [pltpu.VMEM((n, 1, blk), f32), pltpu.VMEM((n, 1, blk), f32), pltpu.VMEM((n, hd, blk), f32)]
    args = (info, starts, q0, q1) + tuple(parts) + tuple(state) + tuple(douts)
    return pl.pallas_call(
        functools.partial(forward_kernel, heads, hd, share, pieces),
        out_shape=shapes,
        in_specs=[sm()] + [vm()] * (len(args) - 1),
        out_specs=(vm(),) * 3,
        scratch_shapes=work,
        compiler_params=params(),
        cost_estimate=pl.CostEstimate(flops=4 * WINDOW * n * blk * blk * hd, bytes_accessed=4 << 20, transcendentals=0),
        name="forward_part",
    )(*args)


def merge_stats(s_mine, s_theirs):
    m = jnp.maximum(s_mine[0:1], s_theirs[0:1])
    fa = jnp.exp2(s_mine[0:1] - m)
    fb = jnp.exp2(s_theirs[0:1] - m)
    total = s_mine[1:2] * fa + s_theirs[1:2] * fb
    delta = (s_mine[2:3] * fa + s_theirs[2:3] * fb) / total
    return m + jnp.log2(total), fa / total, fb / total, delta


def backward_kernel(heads, hd, span, pieces, info_ref, start_ref, q0_ref, q1_ref, d0_ref, d1_ref, sa_ref, sb_ref, *rest):
    blk = q0_ref.shape[0]
    scale = LOG2E / math.sqrt(hd)
    back = 1.0 / math.sqrt(hd)
    parts = 1 + max(piece[0] for piece in pieces)
    part_refs, rest = rest[:parts], rest[parts:]
    if span == "all":
        ga_ref, gb_ref, dq_ref = rest[:3]
        work = rest[3:]
        dq_ref[...] = jnp.zeros(dq_ref.shape, jnp.float32)
    elif span == "half":
        dq_in, ga_ref, gb_ref, dq_ref = rest[:4]
        work = rest[4:]
        dq_ref[...] = dq_in[...]
    else:
        dq_in, mine_ref, theirs_ref, ga_ref, gb_ref, att_ref, dq0_ref, dq1_ref = rest[:8]
        work = rest[8:-1]
        dq_ref = rest[-1]
        dq_ref[...] = dq_in[...]
    q_ref, d_ref, window_ref, grad_ref, log_ref, delta_ref, qs_ref, bias_ref = work
    grad_ref[...] = jnp.zeros(grad_ref.shape, jnp.float32)
    fill(window_ref, part_refs, pieces, blk)
    fill_heads(q_ref, (q0_ref, q1_ref), heads, hd)
    fill_heads(d_ref, (d0_ref, d1_ref), heads, hd)
    fill_scaled(qs_ref, (q0_ref, q1_ref), heads, hd, scale)
    for r in range(2):
        for h in range(heads):
            x = r * heads + h
            log_total, wa, wb, delta = merge_stats(sa_ref[x], sb_ref[(1 - r) * heads + h])
            log_ref[x] = log_total
            delta_ref[x] = delta
            if span == "own" and r == 0:
                att = mine_ref[h] * wa + theirs_ref[h].astype(jnp.float32) * wb
                att_ref[:, h * hd:(h + 1) * hd] = att.T.astype(jnp.bfloat16)

    def tile(j, masks):
        xs = range(2 * heads)
        kb = window_ref[0, j]
        vb = window_ref[1, j]
        kt = kb.T
        qs = [q_ref[x] for x in xs]
        ds = [d_ref[x] for x in xs]
        rows = [(log_ref[x], delta_ref[x]) for x in xs]
        sums = [dq_ref[x] for x in xs]
        dk, dv = grad_ref[0, j], grad_ref[1, j]
        k2 = jnp.concatenate([kb, kb], axis=1)
        found = [nt(k2, qs_ref[x]) for x in xs]
        pushed = [nt(vb, d) for d in ds]
        weights, slopes = [], []
        for x, s, dp, (log_total, delta) in zip(xs, found, pushed, rows):
            if masks is not None:
                s = s + masks[x // heads]
            p = jnp.exp2(s - log_total)
            weights.append(p.astype(jnp.bfloat16))
            slopes.append((p * (dp - delta)).astype(jnp.bfloat16))
        dv = dv + nn(jnp.concatenate(weights, axis=1), jnp.concatenate(ds, axis=0))
        dk = dk + nn(jnp.concatenate(slopes, axis=1), jnp.concatenate(qs, axis=0))
        sums = [dq + nn(kt, slope) for dq, slope in zip(sums, slopes)]
        for x, dq in zip(xs, sums):
            dq_ref[x] = dq
        grad_ref[0, j] = dk
        grad_ref[1, j] = dv

    def pairs(j1, j2):
        xs = range(2 * heads)
        kb = jnp.concatenate([window_ref[0, j1], window_ref[0, j2]], axis=0)
        vb = jnp.concatenate([window_ref[1, j1], window_ref[1, j2]], axis=0)
        kt = kb.T
        qs = [q_ref[x] for x in xs]
        ds = [d_ref[x] for x in xs]
        rows = [(log_ref[x], delta_ref[x]) for x in xs]
        sums = [dq_ref[x] for x in xs]
        k2 = jnp.concatenate([kb, kb], axis=1)
        found = [nt(k2, qs_ref[x]) for x in xs]
        pushed = [nt(vb, d) for d in ds]
        weights, slopes = [], []
        for x, s, dp, (log_total, delta) in zip(xs, found, pushed, rows):
            p = jnp.exp2(s - log_total)
            weights.append(p.astype(jnp.bfloat16))
            slopes.append((p * (dp - delta)).astype(jnp.bfloat16))
        dv = nn(jnp.concatenate(weights, axis=1), jnp.concatenate(ds, axis=0))
        dk = nn(jnp.concatenate(slopes, axis=1), jnp.concatenate(qs, axis=0))
        sums = [dq + nn(kt, slope) for dq, slope in zip(sums, slopes)]
        for x, dq in zip(xs, sums):
            dq_ref[x] = dq
        grad_ref[0, j1] = dk[:blk]
        grad_ref[0, j2] = dk[blk:]
        grad_ref[1, j1] = dv[:blk]
        grad_ref[1, j2] = dv[blk:]

    over_tiles(info_ref, start_ref, bias_ref, blk, span, tile, pairs)
    lists = {"all": ([0, 1, 2, 3, 8], [4, 5, 6, 7, 9]), "half": ([0, 1, 2, 3], [4, 5, 6, 7]), "own": ([0], [1])}
    for chunks, g_ref in zip(lists[span], (ga_ref, gb_ref)):
        for i, j in enumerate(chunks):
            rows = slice(i * blk, (i + 1) * blk)
            g_ref[0, rows, :] = (grad_ref[0, j] * back).astype(jnp.bfloat16)
            g_ref[1, rows, :] = grad_ref[1, j].astype(jnp.bfloat16)
    if span == "own":
        for h in range(heads):
            columns = slice(h * hd, (h + 1) * hd)
            dq0_ref[:, columns] = (dq_ref[h] * back).T
            dq1_ref[:, columns] = (dq_ref[heads + h] * back).T.astype(jnp.bfloat16)


def backward(info, starts, q0, q1, d0, d1, s_mine, s_theirs, parts, pieces, span, sums=()):
    blk, width = q0.shape
    hd = parts[0].shape[2]
    heads = width // hd
    n = 2 * heads
    f32 = jnp.float32
    count = {"all": WINDOW, "half": 2 * HALF, "own": 2}[span]
    grad = jax.ShapeDtypeStruct((2, count // 2 * blk, hd), jnp.bfloat16)
    two = pltpu.VMEM((n, blk, hd), q0.dtype)
    row = pltpu.VMEM((n, 1, blk), f32)
    work = [two, two, pltpu.VMEM((2, count, blk, hd), q0.dtype), pltpu.VMEM((2, count, blk, hd), f32), row, row,
            pltpu.VMEM((n, blk, 2 * hd), q0.dtype), pltpu.VMEM((2, blk, blk), f32)]
    if span == "own":
        out = jax.ShapeDtypeStruct((blk, width), jnp.bfloat16)
        shapes = (grad, grad, out, jax.ShapeDtypeStruct((blk, width), f32), out)
        work += [pltpu.VMEM((n, hd, blk), f32)]
    else:
        shapes = (grad, grad, jax.ShapeDtypeStruct((n, hd, blk), f32))
    args = (info, starts, q0, q1, d0, d1, s_mine, s_theirs) + tuple(parts) + tuple(sums)
    return pl.pallas_call(
        functools.partial(backward_kernel, heads, hd, span, pieces),
        out_shape=shapes,
        in_specs=[sm()] + [vm()] * (len(args) - 1),
        out_specs=(vm(),) * len(shapes),
        scratch_shapes=work,
        compiler_params=params(),
        cost_estimate=pl.CostEstimate(flops=10 * count * n * blk * blk * hd, bytes_accessed=4 << 20, transcendentals=0),
        name="backward_part",
    )(*args)


def per_device(queries, keys, values, dout, doc_lengths):
    blk = queries.shape[0]
    seqs, subs = lax.axis_size("seq"), lax.axis_size("sub")
    seq, sub = lax.axis_index("seq"), lax.axis_index("sub")
    f32, bf16 = jnp.float32, jnp.bfloat16
    chip, core = seq // 2, seq % 2
    mate = sub + 1 - 2 * (sub % 2)
    far = (sub + 2 * (sub % 2) - 1 + subs) % subs
    ids = jnp.stack([chip, core, sub, mate, far]).astype(jnp.int32)
    *infos, starts = tables(ids, doc_lengths, blk, subs)

    def swap_core(value):
        return lax.ppermute(value, "seq", [(s, s ^ 1) for s in range(seqs)])

    def swap_mate(value):
        return lax.ppermute(value, "sub", [(s, s ^ 1) for s in range(subs)])

    def swap_far(value):
        return lax.ppermute(value, "sub", [(s, (s + 2 * (s % 2) - 1) % subs) for s in range(subs)])

    def route(step, sign):
        pairs = [(s, s + 2 * (1 + step + 2 * (s % 2))) for s in range(seqs)]
        return [(a, b)[::sign] for a, b in pairs if b < seqs]

    tie = lax.optimization_barrier
    other_keys, other_values = swap_core(keys), swap_core(values)
    q_mate, d_mate = swap_mate(queries), swap_mate(dout)
    pair = tie(jnp.concatenate([jnp.stack([keys, values]), jnp.stack([other_keys, other_values])], axis=1))
    pair_far = swap_far(pair)
    near = lax.ppermute(pair, "seq", route(0, 1))
    away = lax.ppermute(pair, "seq", route(1, 1))
    near, infos, starts = tie((near, infos, starts))
    near_far = swap_far(near)
    away, q_mate, d_mate, pair_far, near_far = tie((away, q_mate, d_mate, pair_far, near_far))
    most = jnp.concatenate([near, away, near_far], axis=1)
    most_x = swap_core(most)
    away_far = swap_far(away)
    near_pieces = ((0, 0, HALF), (1, 0, HALF), (2, 0, 2))
    far_pieces = ((0, HALF, 2), (2, 0, 2), (1, HALF, 2), (3, 0, 2), (4, 0, 2))
    state = forward(infos[0], starts, queries, q_mate, (most, most_x, pair), near_pieces, 0)
    away_far, state = tie((away_far, state))
    away_far_x = swap_core(away_far)
    far_parts = (most, most_x, away_far, away_far_x, pair_far)
    stats, mine, theirs = forward(infos[1], starts, queries, q_mate, far_parts, far_pieces, 1, state, (dout, d_mate))
    common = (starts, queries, q_mate, dout, d_mate, stats, swap_mate(stats))
    grad_a, grad_b, dq = backward(infos[1], *common, far_parts, far_pieces, "all")
    grad_b, theirs = tie((grad_b, theirs))
    theirs = swap_mate(theirs)
    grad_a = (grad_a.astype(f32) + swap_core(grad_b).astype(f32)).astype(bf16)
    grad_a, dq = tie((grad_a, dq))
    grad_far = swap_far(grad_a)
    grad_a, grad_b, dq = backward(infos[0], *common, (most, most_x), near_pieces[:2], "half", (dq,))
    grad_b, grad_far, theirs = tie((grad_b, grad_far, theirs))
    home = (grad_a.astype(f32) + swap_core(grad_b).astype(f32) + grad_far[:, : HALF * blk].astype(f32)).astype(bf16)
    home, dq = tie((home, dq))
    near = lax.ppermute(home[:, : 2 * blk], "seq", route(0, -1))
    away = lax.ppermute(home[:, 2 * blk :], "seq", route(1, -1))
    grad_own, grad_other, attended, dq_mine, dq_mate = backward(
        infos[0], *common, (pair,), ((0, 0, 2),), "own", (dq, mine, theirs)
    )
    dq_back = swap_mate(dq_mate)
    near, away, grad_own, grad_other = tie((near, away, grad_own, grad_other))
    back = near.astype(f32) + away.astype(f32)
    other = swap_core((back[:, blk:] + grad_other.astype(f32)).astype(bf16))
    query_grad = (dq_mine + dq_back.astype(f32)).astype(bf16)
    total = [
        (grad_own[i].astype(f32) + grad_far[i, HALF * blk :].astype(f32) + back[i, :blk] + other[i].astype(f32)).astype(bf16)
        for i in range(2)
    ]
    return attended, query_grad, total[0], total[1]


def solution(mesh):
    rows = P(("seq", "sub"), None)
    return jax.shard_map(
        per_device,
        mesh=mesh,
        in_specs=(rows, rows, rows, rows, P()),
        out_specs=(rows, rows, rows, rows),
        check_vma=False,
    )
```

profile of v0, /device:TPU:4, one launch (start us, length us, event | category | flops | bytes accessed | tf_op | source)
XLA Modules:
  0.0 107.8 jit_solution(17787277360012049845)
XLA Ops:
  0.6 0.1 collective-permute-start
  0.7 0.5 collective-permute-start.1
  1.2 1.0 collective-permute-done
  2.2 0.2 collective-permute-done.1
  2.3 0.9 maximum_maximum_fusion.rest_2_.rest_0_
  3.3 3.5 %collective-permute-start.2 = (bf16[2,512,128]{2,1,0:T(8,128)(2,1)S(1)}, bf16[2,512,128]{2,1,0:T(8,128)(2,1)S(1)}, u32[]{:S(2)}, u32[]{:S(2)}) collective-permute-start(bf16[2,512,128]{2,1,0:T(8,128)(2,1)S(1)} %maximum_maximum_fusion.rest_2_.rest_0_), channel_id=1, source_target_pairs={{0,8},{4,28},{8,16},{12,36},{16,24},{20,44},{24,32},{28,52},{32,40... | collective-permute-start | bytes 786440 | tf_op jit(solution)/shard_map/ppermute | solution.py:408
  6.8 2.0 %collective-permute-start.5 = (bf16[256,512]{1,0:T(8,128)(2,1)}, bf16[256,512]{1,0:T(8,128)(2,1)S(1)}, u32[]{:S(2)}, u32[]{:S(2)}) collective-permute-start(bf16[256,512]{1,0:T(8,128)(2,1)} %d0_ref.5), channel_id=1, source_target_pairs={{0,1},{1,0},{2,3},{3,2},{4,5},{5,4},{6,7},{7,6},{8,9},{9,8},{10,11... | collective-permute-start | bytes 786440 | tf_op jit(solution)/shard_map/ppermute | solution.py:394
  8.8 0.1 collective-permute-start.4
  8.9 0.7 stack.47.ids_ref
  9.5 1.6 %tile_tables.1 = (s32[36]{0:T(128)}, s32[36]{0:T(128)}, s32[2,1,256]{2,1,0:T(1,128)}) custom-call(s32[5]{0:T(128)} %stack.47.ids_ref, s32[32]{0:T(128)} %len_ref.1), custom_call_target="tpu_custom_call" | custom-call | tf_op jit(solution)/shard_map/tile_tables/pallas_call | solution.py:70
  11.2 0.0 copy-start.2
  11.2 0.0 copy-start.3
  11.2 4.1 %collective-permute-start.6 = (bf16[2,512,128]{2,1,0:T(8,128)(2,1)S(1)}, bf16[2,512,128]{2,1,0:T(8,128)(2,1)S(1)}, u32[]{:S(2)}, u32[]{:S(2)}) collective-permute-start(bf16[2,512,128]{2,1,0:T(8,128)(2,1)S(1)} %maximum_maximum_fusion.rest_2_.rest_0_), channel_id=1, source_target_pairs={{0,3},{1,2},{2,1},{3,0},{4,7},{5,6},{6,5},{7,4},{8,11},{9,10},{10,... | collective-permute-start | bytes 786440 | tf_op jit(solution)/shard_map/ppermute | solution.py:397
  15.3 4.8 %collective-permute-start.3 = (bf16[2,512,128]{2,1,0:T(8,128)(2,1)S(1)}, bf16[2,512,128]{2,1,0:T(8,128)(2,1)S(1)}, u32[]{:S(2)}, u32[]{:S(2)}) collective-permute-start(bf16[2,512,128]{2,1,0:T(8,128)(2,1)S(1)} %maximum_maximum_fusion.rest_2_.rest_0_), channel_id=1, source_target_pairs={{0,16},{4,36},{8,24},{12,44},{16,32},{20,52},{24,40},{28,60},{32,4... | collective-permute-start | bytes 786440 | tf_op jit(solution)/shard_map/ppermute | solution.py:409
  20.1 0.3 collective-permute-start.7
  20.4 0.7 collective-permute-done.4.q1_ref
  21.2 1.0 collective-permute-done.6.rest_4_
  22.2 4.6 %collective-permute-done.3 = bf16[2,512,128]{2,1,0:T(8,128)(2,1)S(1)} collective-permute-done((bf16[2,512,128]{2,1,0:T(8,128)(2,1)S(1)}, bf16[2,512,128]{2,1,0:T(8,128)(2,1)S(1)}, u32[]{:S(2)}, u32[]{:S(2)}) %collective-permute-start.3) | collective-permute-done | bytes 262176 | tf_op jit(solution)/shard_map/ppermute | solution.py:409
  26.8 1.5 %collective-permute-done.7 = bf16[2,512,128]{2,1,0:T(8,128)(2,1)S(1)} collective-permute-done((bf16[2,512,128]{2,1,0:T(8,128)(2,1)S(1)}, bf16[2,512,128]{2,1,0:T(8,128)(2,1)S(1)}, u32[]{:S(2)}, u32[]{:S(2)}) %collective-permute-start.7) | collective-permute-done | bytes 262176 | tf_op jit(solution)/shard_map/ppermute | solution.py:397
  28.4 0.0 copy-start.1
  28.4 0.0 copy-start.4
  28.4 0.1 collective-permute-start.8
  28.5 3.1 %collective-permute-start.9 = (bf16[2,512,128]{2,1,0:T(8,128)(2,1)S(1)}, bf16[2,512,128]{2,1,0:T(8,128)(2,1)S(1)}, u32[]{:S(2)}, u32[]{:S(2)}) collective-permute-start(bf16[2,512,128]{2,1,0:T(8,128)(2,1)S(1)} %collective-permute-done.3), channel_id=1, source_target_pairs={{0,3},{1,2},{2,1},{3,0},{4,7},{5,6},{6,5},{7,4},{8,11},{9,10},{10,... | collective-permute-start | bytes 786440 | tf_op jit(solution)/shard_map/ppermute | solution.py:397
  31.6 1.9 %forward_part.2 = (f32[8,1,256]{2,1,0:T(1,128)S(1)}, f32[8,1,256]{2,1,0:T(1,128)S(1)}, f32[8,128,256]{2,1,0:T(8,128)S(1)}) custom-call(s32[36]{0:T(128)S(1)} %copy-done.3, s32[2,1,256]{2,1,0:T(1,128)S(1)} %copy-done.2, bf16[256,512]{1,0:T(8,128)(2,1)S(1)} %copy-done, bf16[256,512]{1,0:T(8,128)(2,1)S(1)} %collective-permute-done.4.q1_ref, ...), custom_call_target="tpu_custom_call" | custom-call | flops 2684354560 | bytes 4194304 | tf_op jit(solution)/shard_map/forward_part/pallas_call | solution.py:223
  33.5 5.0 %collective-permute-done.9.rest_2_ = bf16[2,512,128]{2,1,0:T(8,128)(2,1)S(1)} collective-permute-done((bf16[2,512,128]{2,1,0:T(8,128)(2,1)S(1)}, bf16[2,512,128]{2,1,0:T(8,128)(2,1)S(1)}, u32[]{:S(2)}, u32[]{:S(2)}) %collective-permute-start.9) | collective-permute-done | bytes 262176 | tf_op jit(solution)/shard_map/ppermute | solution.py:397
  38.5 1.5 %collective-permute-done.10.rest_3_ = bf16[2,512,128]{2,1,0:T(8,128)(2,1)S(1)} collective-permute-done((bf16[2,512,128]{2,1,0:T(8,128)(2,1)S(1)}, bf16[2,512,128]{2,1,0:T(8,128)(2,1)S(1)}, u32[]{:S(2)}, u32[]{:S(2)}) %collective-permute-start.10) | collective-permute-done | bytes 262176 | tf_op jit(solution)/shard_map/ppermute | solution.py:391
  40.0 2.1 %forward_part.3 = (f32[8,3,256]{2,1,0:T(4,128)S(1)}, f32[4,128,256]{2,1,0:T(8,128)S(1)}, bf16[4,128,256]{2,1,0:T(8,128)(2,1)S(1)}) custom-call(s32[36]{0:T(128)S(1)} %copy-done.4, s32[2,1,256]{2,1,0:T(1,128)S(1)} %copy-done.2, bf16[256,512]{1,0:T(8,128)(2,1)S(1)} %copy-done, bf16[256,512]{1,0:T(8,128)(2,1)S(1)} %collective-permute-done.4.q1_ref, ...), custom_call_target="tpu_custom_call" | custom-call | flops 2684354560 | bytes 4194304 | tf_op jit(solution)/shard_map/forward_part/pallas_call | solution.py:223
  42.1 0.1 collective-permute-start.11
  42.2 3.9 %collective-permute-done.11.sb_ref = f32[8,3,256]{2,1,0:T(4,128)S(1)} collective-permute-done((f32[8,3,256]{2,1,0:T(4,128)S(1)}, f32[8,3,256]{2,1,0:T(4,128)S(1)}, u32[]{:S(2)}, u32[]{:S(2)}) %collective-permute-start.11) | collective-permute-done | bytes 24608 | tf_op jit(solution)/shard_map/ppermute | solution.py:394
  46.1 3.2 %backward_part.3 = (bf16[2,1280,128]{2,1,0:T(8,128)(2,1)S(1)}, bf16[2,1280,128]{2,1,0:T(8,128)(2,1)S(1)}, f32[8,128,256]{2,1,0:T(8,128)S(1)}) custom-call(s32[36]{0:T(128)S(1)} %copy-done.4, s32[2,1,256]{2,1,0:T(1,128)S(1)} %copy-done.2, bf16[256,512]{1,0:T(8,128)(2,1)S(1)} %copy-done, bf16[256,512]{1,0:T(8,128)(2,1)S(1)} %collective-permute-done.4.q1_ref, ...), custom_call_target="tpu_custom_call" | custom-call | flops 6710886400 | bytes 4194304 | tf_op jit(solution)/shard_map/backward_part/pallas_call | solution.py:367
  49.4 0.1 collective-permute-start.12
  49.5 2.1 %collective-permute-done.12 = bf16[2,1280,128]{2,1,0:T(8,128)(2,1)S(1)} collective-permute-done((bf16[2,1280,128]{2,1,0:T(8,128)(2,1)S(1)}, bf16[2,1280,128]{2,1,0:T(8,128)(2,1)S(1)}, u32[]{:S(2)}, u32[]{:S(2)}) %collective-permute-start.12) | collective-permute-done | bytes 655392 | tf_op jit(solution)/shard_map/ppermute | solution.py:391
  51.6 0.2 add_convert_fusion
  51.7 2.0 %collective-permute-start.13 = (bf16[2,1280,128]{2,1,0:T(8,128)(2,1)S(1)}, bf16[2,1280,128]{2,1,0:T(8,128)(2,1)S(1)}, u32[]{:S(2)}, u32[]{:S(2)}) collective-permute-start(bf16[2,1280,128]{2,1,0:T(8,128)(2,1)S(1)} %add_convert_fusion), channel_id=1, source_target_pairs={{0,3},{1,2},{2,1},{3,0},{4,7},{5,6},{6,5},{7,4},{8,11},{9,10},{10,... | collective-permute-start | bytes 1966088 | tf_op jit(solution)/shard_map/ppermute | solution.py:397
  53.8 1.6 %backward_part.4 = (bf16[2,1024,128]{2,1,0:T(8,128)(2,1)S(1)}, bf16[2,1024,128]{2,1,0:T(8,128)(2,1)S(1)}, f32[8,128,256]{2,1,0:T(8,128)S(1)}) custom-call(s32[36]{0:T(128)S(1)} %copy-done.3, s32[2,1,256]{2,1,0:T(1,128)S(1)} %copy-done.2, bf16[256,512]{1,0:T(8,128)(2,1)S(1)} %copy-done, bf16[256,512]{1,0:T(8,128)(2,1)S(1)} %collective-permute-done.4.q1_ref, ...), custom_call_target="tpu_custom_call" | custom-call | flops 5368709120 | bytes 4194304 | tf_op jit(solution)/shard_map/backward_part/pallas_call | solution.py:367
  55.4 6.7 %collective-permute-done.14.rest_3_ = bf16[4,128,256]{2,1,0:T(8,128)(2,1)S(1)} collective-permute-done((bf16[4,128,256]{2,1,0:T(8,128)(2,1)S(1)}, bf16[4,128,256]{2,1,0:T(8,128)(2,1)S(1)}, u32[]{:S(2)}, u32[]{:S(2)}) %collective-permute-start.14) | collective-permute-done | bytes 262176 | tf_op jit(solution)/shard_map/ppermute | solution.py:394
  62.1 7.7 %collective-permute-done.13 = bf16[2,1280,128]{2,1,0:T(8,128)(2,1)S(1)} collective-permute-done((bf16[2,1280,128]{2,1,0:T(8,128)(2,1)S(1)}, bf16[2,1280,128]{2,1,0:T(8,128)(2,1)S(1)}, u32[]{:S(2)}, u32[]{:S(2)}) %collective-permute-start.13) | collective-permute-done | bytes 655392 | tf_op jit(solution)/shard_map/ppermute | solution.py:397
  69.8 1.9 %collective-permute-done.15 = bf16[2,1024,128]{2,1,0:T(8,128)(2,1)S(1)} collective-permute-done((bf16[2,1024,128]{2,1,0:T(8,128)(2,1)S(1)}, bf16[2,1024,128]{2,1,0:T(8,128)(2,1)S(1)}, u32[]{:S(2)}, u32[]{:S(2)}) %collective-permute-start.15) | collective-permute-done | bytes 524320 | tf_op jit(solution)/shard_map/ppermute | solution.py:391
  71.7 0.2 add_convert_fusion.1
  72.0 12.3 %collective-permute-start.18 = (bf16[2,512,128]{2,1,0:T(8,128)(2,1)S(1)}, bf16[2,512,128]{2,1,0:T(8,128)(2,1)S(1)}, u32[]{:S(2)}, u32[]{:S(2)}) collective-permute-start(bf16[2,512,128]{2,1,0:T(8,128)(2,1)S(1)} %get-tuple-element.98), channel_id=1, source_target_pairs={{16,0},{36,4},{24,8},{44,12},{32,16},{52,20},{40,24},{60,28},{48,3... | collective-permute-start | bytes 786440 | tf_op jit(solution)/shard_map/ppermute | solution.py:435
  84.3 12.1 %collective-permute-start.17 = (bf16[2,512,128]{2,1,0:T(8,128)(2,1)S(1)}, bf16[2,512,128]{2,1,0:T(8,128)(2,1)S(1)}, u32[]{:S(2)}, u32[]{:S(2)}) collective-permute-start(bf16[2,512,128]{2,1,0:T(8,128)(2,1)S(1)} %get-tuple-element.99), channel_id=1, source_target_pairs={{8,0},{28,4},{16,8},{36,12},{24,16},{44,20},{32,24},{52,28},{40,32... | collective-permute-start | bytes 786440 | tf_op jit(solution)/shard_map/ppermute | solution.py:434
  96.3 3.6 %backward_part.5 = (bf16[2,256,128]{2,1,0:T(8,128)(2,1)S(1)}, bf16[2,256,128]{2,1,0:T(8,128)(2,1)S(1)}, bf16[256,512]{1,0:T(8,128)(2,1)}, f32[256,512]{1,0:T(8,128)S(1)}, bf16[256,512]{1,0:T(8,128)(2,1)S(1)}) custom-call(s32[36]{0:T(128)S(1)} %copy-done.3, s32[2,1,256]{2,1,0:T(1,128)S(1)} %copy-done.2, bf16[256,512]{1,0:T(8,128)(2,1)S(1)} %copy-done, ...), custom_call_target="tpu_custom_call" | custom-call | flops 1342177280 | bytes 4194304 | tf_op jit(solution)/shard_map/backward_part/pallas_call | solution.py:367
  99.9 1.6 %collective-permute-done.17 = bf16[2,512,128]{2,1,0:T(8,128)(2,1)S(1)} collective-permute-done((bf16[2,512,128]{2,1,0:T(8,128)(2,1)S(1)}, bf16[2,512,128]{2,1,0:T(8,128)(2,1)S(1)}, u32[]{:S(2)}, u32[]{:S(2)}) %collective-permute-start.17) | collective-permute-done | bytes 262176 | tf_op jit(solution)/shard_map/ppermute | solution.py:434
  101.5 0.1 convert_add_fusion
  101.6 0.1 collective-permute-start.19
  101.7 4.6 %collective-permute-done.16 = bf16[256,512]{1,0:T(8,128)(2,1)S(1)} collective-permute-done((bf16[256,512]{1,0:T(8,128)(2,1)S(1)}, bf16[256,512]{1,0:T(8,128)(2,1)S(1)}, u32[]{:S(2)}, u32[]{:S(2)}) %collective-permute-start.16) | collective-permute-done | bytes 262176 | tf_op jit(solution)/shard_map/ppermute | solution.py:394
  106.3 0.8 add_convert_fusion.2
  107.1 0.7 fusion.6
  (20 shorter events, 0.2 us)
Async XLA Ops:
  0.6 1.5 %collective-permute-start = (bf16[256,128]{1,0:T(8,128)(2,1)}, bf16[256,128]{1,0:T(8,128)(2,1)S(1)}, u32[]{:S(2)}, u32[]{:S(2)}) collective-permute-start(bf16[256,128]{1,0:T(8,128)(2,1)} %param.6), channel_id=1, source_target_pairs={{0,4},{4,0},{8,12},{12,8},{16,20},{20,16},{24,28},{28,24},{32,36},... | collective-permute-start | bytes 196616 | tf_op jit(solution)/shard_map/ppermute | solution.py:391
  0.7 1.6 %collective-permute-start.1 = (bf16[256,128]{1,0:T(8,128)(2,1)}, bf16[256,128]{1,0:T(8,128)(2,1)S(1)}, u32[]{:S(2)}, u32[]{:S(2)}) collective-permute-start(bf16[256,128]{1,0:T(8,128)(2,1)} %param.7), channel_id=1, source_target_pairs={{0,4},{4,0},{8,12},{12,8},{16,20},{20,16},{24,28},{28,24},{32,36},... | collective-permute-start | bytes 196616 | tf_op jit(solution)/shard_map/ppermute | solution.py:391
  2.3 29.2 %copy-start = (bf16[256,512]{1,0:T(8,128)(2,1)S(1)}, bf16[256,512]{1,0:T(8,128)(2,1)}, u32[]{:S(2)}) copy-start(bf16[256,512]{1,0:T(8,128)(2,1)} %q0_ref.9) | copy-start | bytes 786436
  3.3 16.8 %collective-permute-start.2 = (bf16[2,512,128]{2,1,0:T(8,128)(2,1)S(1)}, bf16[2,512,128]{2,1,0:T(8,128)(2,1)S(1)}, u32[]{:S(2)}, u32[]{:S(2)}) collective-permute-start(bf16[2,512,128]{2,1,0:T(8,128)(2,1)S(1)} %maximum_maximum_fusion.rest_2_.rest_0_), channel_id=1, source_target_pairs={{0,8},{4,28},{8,16},{12,36},{16,24},{20,44},{24,32},{28,52},{32,40... | collective-permute-start | bytes 786440 | tf_op jit(solution)/shard_map/ppermute | solution.py:408
  6.8 13.7 %collective-permute-start.5 = (bf16[256,512]{1,0:T(8,128)(2,1)}, bf16[256,512]{1,0:T(8,128)(2,1)S(1)}, u32[]{:S(2)}, u32[]{:S(2)}) collective-permute-start(bf16[256,512]{1,0:T(8,128)(2,1)} %d0_ref.5), channel_id=1, source_target_pairs={{0,1},{1,0},{2,3},{3,2},{4,5},{5,4},{6,7},{7,6},{8,9},{9,8},{10,11... | collective-permute-start | bytes 786440 | tf_op jit(solution)/shard_map/ppermute | solution.py:394
  8.8 12.4 %collective-permute-start.4 = (bf16[256,512]{1,0:T(8,128)(2,1)}, bf16[256,512]{1,0:T(8,128)(2,1)S(1)}, u32[]{:S(2)}, u32[]{:S(2)}) collective-permute-start(bf16[256,512]{1,0:T(8,128)(2,1)} %q0_ref.9), channel_id=1, source_target_pairs={{0,1},{1,0},{2,3},{3,2},{4,5},{5,4},{6,7},{7,6},{8,9},{9,8},{10,11... | collective-permute-start | bytes 786440 | tf_op jit(solution)/shard_map/ppermute | solution.py:394
  11.2 20.4 %copy-start.2 = (s32[2,1,256]{2,1,0:T(1,128)S(1)}, s32[2,1,256]{2,1,0:T(1,128)}, u32[]{:S(2)}) copy-start(s32[2,1,256]{2,1,0:T(1,128)} %get-tuple-element.54.start_ref) | copy-start | bytes 6148
  11.2 20.4 %copy-start.3 = (s32[36]{0:T(128)S(1)}, s32[36]{0:T(128)}, u32[]{:S(2)}) copy-start(s32[36]{0:T(128)} %get-tuple-element.53.info_ref) | copy-start | bytes 436
  11.2 11.0 %collective-permute-start.6 = (bf16[2,512,128]{2,1,0:T(8,128)(2,1)S(1)}, bf16[2,512,128]{2,1,0:T(8,128)(2,1)S(1)}, u32[]{:S(2)}, u32[]{:S(2)}) collective-permute-start(bf16[2,512,128]{2,1,0:T(8,128)(2,1)S(1)} %maximum_maximum_fusion.rest_2_.rest_0_), channel_id=1, source_target_pairs={{0,3},{1,2},{2,1},{3,0},{4,7},{5,6},{6,5},{7,4},{8,11},{9,10},{10,... | collective-permute-start | bytes 786440 | tf_op jit(solution)/shard_map/ppermute | solution.py:397
  15.3 11.5 %collective-permute-start.3 = (bf16[2,512,128]{2,1,0:T(8,128)(2,1)S(1)}, bf16[2,512,128]{2,1,0:T(8,128)(2,1)S(1)}, u32[]{:S(2)}, u32[]{:S(2)}) collective-permute-start(bf16[2,512,128]{2,1,0:T(8,128)(2,1)S(1)} %maximum_maximum_fusion.rest_2_.rest_0_), channel_id=1, source_target_pairs={{0,16},{4,36},{8,24},{12,44},{16,32},{20,52},{24,40},{28,60},{32,4... | collective-permute-start | bytes 786440 | tf_op jit(solution)/shard_map/ppermute | solution.py:409
  20.1 8.2 %collective-permute-start.7 = (bf16[2,512,128]{2,1,0:T(8,128)(2,1)S(1)}, bf16[2,512,128]{2,1,0:T(8,128)(2,1)S(1)}, u32[]{:S(2)}, u32[]{:S(2)}) collective-permute-start(bf16[2,512,128]{2,1,0:T(8,128)(2,1)S(1)} %collective-permute-done.2), channel_id=1, source_target_pairs={{0,3},{1,2},{2,1},{3,0},{4,7},{5,6},{6,5},{7,4},{8,11},{9,10},{10,... | collective-permute-start | bytes 786440 | tf_op jit(solution)/shard_map/ppermute | solution.py:397
  28.4 11.6 %copy-start.1 = (bf16[256,512]{1,0:T(8,128)(2,1)S(1)}, bf16[256,512]{1,0:T(8,128)(2,1)}, u32[]{:S(2)}) copy-start(bf16[256,512]{1,0:T(8,128)(2,1)} %d0_ref.5) | copy-start | bytes 786436
  28.4 11.6 %copy-start.4 = (s32[36]{0:T(128)S(1)}, s32[36]{0:T(128)}, u32[]{:S(2)}) copy-start(s32[36]{0:T(128)} %get-tuple-element.58.info_ref) | copy-start | bytes 436
  28.4 3.2 %collective-permute-start.8 = (bf16[2,1536,128]{2,1,0:T(8,128)(2,1)S(1)}, bf16[2,1536,128]{2,1,0:T(8,128)(2,1)S(1)}, u32[]{:S(2)}, u32[]{:S(2)}) collective-permute-start(bf16[2,1536,128]{2,1,0:T(8,128)(2,1)S(1)} %constant_dynamic-update-slice_fusion.rest_0_), channel_id=1, source_target_pairs={{0,4},{4,0},{8,12},{12,8},{16,20},{20,16},{24,28},{28,24},{32,36},... | collective-permute-start | bytes 2359304 | tf_op jit(solution)/shard_map/ppermute | solution.py:391
  28.5 9.9 %collective-permute-start.9 = (bf16[2,512,128]{2,1,0:T(8,128)(2,1)S(1)}, bf16[2,512,128]{2,1,0:T(8,128)(2,1)S(1)}, u32[]{:S(2)}, u32[]{:S(2)}) collective-permute-start(bf16[2,512,128]{2,1,0:T(8,128)(2,1)S(1)} %collective-permute-done.3), channel_id=1, source_target_pairs={{0,3},{1,2},{2,1},{3,0},{4,7},{5,6},{6,5},{7,4},{8,11},{9,10},{10,... | collective-permute-start | bytes 786440 | tf_op jit(solution)/shard_map/ppermute | solution.py:397
  38.4 1.5 %collective-permute-start.10 = (bf16[2,512,128]{2,1,0:T(8,128)(2,1)S(1)}, bf16[2,512,128]{2,1,0:T(8,128)(2,1)S(1)}, u32[]{:S(2)}, u32[]{:S(2)}) collective-permute-start(bf16[2,512,128]{2,1,0:T(8,128)(2,1)S(1)} %collective-permute-done.9.rest_2_), channel_id=1, source_target_pairs={{0,4},{4,0},{8,12},{12,8},{16,20},{20,16},{24,28},{28,24},{32,36},... | collective-permute-start | bytes 786440 | tf_op jit(solution)/shard_map/ppermute | solution.py:391
  42.1 4.0 %collective-permute-start.11 = (f32[8,3,256]{2,1,0:T(4,128)S(1)}, f32[8,3,256]{2,1,0:T(4,128)S(1)}, u32[]{:S(2)}, u32[]{:S(2)}) collective-permute-start(f32[8,3,256]{2,1,0:T(4,128)S(1)} %get-tuple-element.69.sa_ref), channel_id=1, source_target_pairs={{0,1},{1,0},{2,3},{3,2},{4,5},{5,4},{6,7},{7,6},{8,9},{9,8},{10,11... | collective-permute-start | bytes 73736 | tf_op jit(solution)/shard_map/ppermute | solution.py:394
  49.4 2.2 %collective-permute-start.12 = (bf16[2,1280,128]{2,1,0:T(8,128)(2,1)S(1)}, bf16[2,1280,128]{2,1,0:T(8,128)(2,1)S(1)}, u32[]{:S(2)}, u32[]{:S(2)}) collective-permute-start(bf16[2,1280,128]{2,1,0:T(8,128)(2,1)S(1)} %get-tuple-element.73), channel_id=1, source_target_pairs={{0,4},{4,0},{8,12},{12,8},{16,20},{20,16},{24,28},{28,24},{32,36},... | collective-permute-start | bytes 1966088 | tf_op jit(solution)/shard_map/ppermute | solution.py:391
  51.7 18.1 %collective-permute-start.13 = (bf16[2,1280,128]{2,1,0:T(8,128)(2,1)S(1)}, bf16[2,1280,128]{2,1,0:T(8,128)(2,1)S(1)}, u32[]{:S(2)}, u32[]{:S(2)}) collective-permute-start(bf16[2,1280,128]{2,1,0:T(8,128)(2,1)S(1)} %add_convert_fusion), channel_id=1, source_target_pairs={{0,3},{1,2},{2,1},{3,0},{4,7},{5,6},{6,5},{7,4},{8,11},{9,10},{10,... | collective-permute-start | bytes 1966088 | tf_op jit(solution)/shard_map/ppermute | solution.py:397
  53.8 8.3 %collective-permute-start.14 = (bf16[4,128,256]{2,1,0:T(8,128)(2,1)S(1)}, bf16[4,128,256]{2,1,0:T(8,128)(2,1)S(1)}, u32[]{:S(2)}, u32[]{:S(2)}) collective-permute-start(bf16[4,128,256]{2,1,0:T(8,128)(2,1)S(1)} %get-tuple-element.79), channel_id=1, source_target_pairs={{0,1},{1,0},{2,3},{3,2},{4,5},{5,4},{6,7},{7,6},{8,9},{9,8},{10,11... | collective-permute-start | bytes 786440 | tf_op jit(solution)/shard_map/ppermute | solution.py:394
  69.8 1.9 %collective-permute-start.15 = (bf16[2,1024,128]{2,1,0:T(8,128)(2,1)S(1)}, bf16[2,1024,128]{2,1,0:T(8,128)(2,1)S(1)}, u32[]{:S(2)}, u32[]{:S(2)}) collective-permute-start(bf16[2,1024,128]{2,1,0:T(8,128)(2,1)S(1)} %get-tuple-element.80), channel_id=1, source_target_pairs={{0,4},{4,0},{8,12},{12,8},{16,20},{20,16},{24,28},{28,24},{32,36},... | collective-permute-start | bytes 1572872 | tf_op jit(solution)/shard_map/ppermute | solution.py:391
  72.0 27.9 %collective-permute-start.18 = (bf16[2,512,128]{2,1,0:T(8,128)(2,1)S(1)}, bf16[2,512,128]{2,1,0:T(8,128)(2,1)S(1)}, u32[]{:S(2)}, u32[]{:S(2)}) collective-permute-start(bf16[2,512,128]{2,1,0:T(8,128)(2,1)S(1)} %get-tuple-element.98), channel_id=1, source_target_pairs={{16,0},{36,4},{24,8},{44,12},{32,16},{52,20},{40,24},{60,28},{48,3... | collective-permute-start | bytes 786440 | tf_op jit(solution)/shard_map/ppermute | solution.py:435
  84.3 17.2 %collective-permute-start.17 = (bf16[2,512,128]{2,1,0:T(8,128)(2,1)S(1)}, bf16[2,512,128]{2,1,0:T(8,128)(2,1)S(1)}, u32[]{:S(2)}, u32[]{:S(2)}) collective-permute-start(bf16[2,512,128]{2,1,0:T(8,128)(2,1)S(1)} %get-tuple-element.99), channel_id=1, source_target_pairs={{8,0},{28,4},{16,8},{36,12},{24,16},{44,20},{32,24},{52,28},{40,32... | collective-permute-start | bytes 786440 | tf_op jit(solution)/shard_map/ppermute | solution.py:434
  99.9 6.4 %collective-permute-start.16 = (bf16[256,512]{1,0:T(8,128)(2,1)S(1)}, bf16[256,512]{1,0:T(8,128)(2,1)S(1)}, u32[]{:S(2)}, u32[]{:S(2)}) collective-permute-start(bf16[256,512]{1,0:T(8,128)(2,1)S(1)} %get-tuple-element.88), channel_id=1, source_target_pairs={{0,1},{1,0},{2,3},{3,2},{4,5},{5,4},{6,7},{7,6},{8,9},{9,8},{10,11... | collective-permute-start | bytes 786440 | tf_op jit(solution)/shard_map/ppermute | solution.py:394
  101.6 5.4 %collective-permute-start.19 = (bf16[2,256,128]{2,1,0:T(8,128)(2,1)S(1)}, bf16[2,256,128]{2,1,0:T(8,128)(2,1)S(1)}, u32[]{:S(2)}, u32[]{:S(2)}) collective-permute-start(bf16[2,256,128]{2,1,0:T(8,128)(2,1)S(1)} %fusion), channel_id=1, source_target_pairs={{0,4},{4,0},{8,12},{12,8},{16,20},{20,16},{24,28},{28,24},{32,36},... | collective-permute-start | bytes 393224 | tf_op jit(solution)/shard_map/ppermute | solution.py:391
where the time goes:
time: 108 us
  starting transfers between devices  45.2 us (42%)
  waiting for transfers between devices  44 us (41%)
  Pallas kernels  14 us (13%)
  other arithmetic  2.91 us (3%)
    ppermute x5, waiting for transfers between devices, swap_mate(): return lax.ppermute(value, 'sub', [(s, s ^ 1) for s in range(subs)])  15.9 us
    ppermute x4, waiting for transfers between devices, swap_far(): lax.ppermute(value, 'sub', [(s, (s + 2 * (s % 2) - 1) % subs) for s in ra...  15.2 us
    ppermute x1, starting transfers between devices, per_device(): away = lax.ppermute(home[:, 2 * blk:], 'seq', route(1, -1))  12.3 us
    ppermute x1, starting transfers between devices, per_device(): near = lax.ppermute(home[:, :2 * blk], 'seq', route(0, -1))  12.1 us
    ppermute x4, starting transfers between devices, swap_far(): lax.ppermute(value, 'sub', [(s, (s + 2 * (s % 2) - 1) % subs) for s in ra...  9.51 us
    pallas_call x3, Pallas kernels, backward(): pl.pallas_call(functools.partial(backward_kernel, heads, hd, span, pieces...  8.41 us
    ppermute x7, waiting for transfers between devices, swap_core(): return lax.ppermute(value, 'seq', [(s, s ^ 1) for s in range(seqs)])  6.64 us
    ppermute x1, starting transfers between devices, per_device(): away = lax.ppermute(pair, 'seq', route(1, 1))  4.8 us
  transfers between devices with their start and end apart: 20, of which 15 were waited for; matrix products, arithmetic and copies ran while one was open for 1% of the time, Pallas kernels for 8%

commit v1 on v0

--- a/solution.py
+++ b/solution.py
@@ -256,8 +256,8 @@
         work = rest[4:]
         dq_ref[...] = dq_in[...]
     else:
-        dq_in, mine_ref, theirs_ref, ga_ref, gb_ref, att_ref, dq0_ref, dq1_ref = rest[:8]
-        work = rest[8:-1]
+        dq_in, ga_ref, gb_ref, dq_out, send_ref = rest[:5]
+        work = rest[5:-1]
         dq_ref = rest[-1]
         dq_ref[...] = dq_in[...]
     q_ref, d_ref, window_ref, grad_ref, log_ref, delta_ref, qs_ref, bias_ref = work
@@ -269,12 +269,9 @@
     for r in range(2):
         for h in range(heads):
             x = r * heads + h
-            log_total, wa, wb, delta = merge_stats(sa_ref[x], sb_ref[(1 - r) * heads + h])
+            log_total, _, _, delta = merge_stats(sa_ref[x], sb_ref[(1 - r) * heads + h])
             log_ref[x] = log_total
             delta_ref[x] = delta
-            if span == "own" and r == 0:
-                att = mine_ref[h] * wa + theirs_ref[h].astype(jnp.float32) * wb
-                att_ref[:, h * hd:(h + 1) * hd] = att.T.astype(jnp.bfloat16)
 
     def tile(j, masks):
         xs = range(2 * heads)
@@ -339,10 +336,8 @@
             g_ref[0, rows, :] = (grad_ref[0, j] * back).astype(jnp.bfloat16)
             g_ref[1, rows, :] = grad_ref[1, j].astype(jnp.bfloat16)
     if span == "own":
-        for h in range(heads):
-            columns = slice(h * hd, (h + 1) * hd)
-            dq0_ref[:, columns] = (dq_ref[h] * back).T
-            dq1_ref[:, columns] = (dq_ref[heads + h] * back).T.astype(jnp.bfloat16)
+        dq_out[...] = dq_ref[:heads]
+        send_ref[...] = (dq_ref[heads:] * back).astype(jnp.bfloat16)
 
 
 def backward(info, starts, q0, q1, d0, d1, s_mine, s_theirs, parts, pieces, span, sums=()):
@@ -358,8 +353,8 @@
     work = [two, two, pltpu.VMEM((2, count, blk, hd), q0.dtype), pltpu.VMEM((2, count, blk, hd), f32), row, row,
             pltpu.VMEM((n, blk, 2 * hd), q0.dtype), pltpu.VMEM((2, blk, blk), f32)]
     if span == "own":
-        out = jax.ShapeDtypeStruct((blk, width), jnp.bfloat16)
-        shapes = (grad, grad, out, jax.ShapeDtypeStruct((blk, width), f32), out)
+        shapes = (grad, grad, jax.ShapeDtypeStruct((heads, hd, blk), f32),
+                  jax.ShapeDtypeStruct((heads, hd, blk), jnp.bfloat16))
         work += [pltpu.VMEM((n, hd, blk), f32)]
     else:
         shapes = (grad, grad, jax.ShapeDtypeStruct((n, hd, blk), f32))
@@ -376,6 +371,31 @@
     )(*args)
 
 
+def output_kernel(heads, hd, sa_ref, sb_ref, mine_ref, theirs_ref, att_ref):
+    for h in range(heads):
+        _, wa, wb, _ = merge_stats(sa_ref[h], sb_ref[heads + h])
+        att = mine_ref[h] * wa + theirs_ref[h].astype(jnp.float32) * wb
+        att_ref[:, h * hd:(h + 1) * hd] = att.T.astype(jnp.bfloat16)
+
+
+def query_grad_kernel(heads, hd, mine_ref, theirs_ref, out_ref):
+    back = 1.0 / math.sqrt(hd)
+    for h in range(heads):
+        total = mine_ref[h] * back + theirs_ref[h].astype(jnp.float32)
+        out_ref[:, h * hd:(h + 1) * hd] = total.T.astype(jnp.bfloat16)
+
+
+def finish(kernel, name, *args):
+    heads, hd, blk = args[-1].shape
+    return pl.pallas_call(
+        functools.partial(kernel, heads, hd),
+        out_shape=jax.ShapeDtypeStruct((blk, heads * hd), jnp.bfloat16),
+        in_specs=[vm()] * len(args),
+        out_specs=vm(),
+        name=name,
+    )(*args)
+
+
 def per_device(queries, keys, values, dout, doc_lengths):
     blk = queries.shape[0]
     seqs, subs = lax.axis_size("seq"), lax.axis_size("sub")
@@ -384,9 +404,6 @@
     chip, core = seq // 2, seq % 2
     mate = sub + 1 - 2 * (sub % 2)
     far = (sub + 2 * (sub % 2) - 1 + subs) % subs
-    ids = jnp.stack([chip, core, sub, mate, far]).astype(jnp.int32)
-    *infos, starts = tables(ids, doc_lengths, blk, subs)
-
     def swap_core(value):
         return lax.ppermute(value, "seq", [(s, s ^ 1) for s in range(seqs)])
 
@@ -402,12 +419,15 @@
 
     tie = lax.optimization_barrier
     other_keys, other_values = swap_core(keys), swap_core(values)
-    q_mate, d_mate = swap_mate(queries), swap_mate(dout)
-    pair = tie(jnp.concatenate([jnp.stack([keys, values]), jnp.stack([other_keys, other_values])], axis=1))
-    pair_far = swap_far(pair)
+    ids = jnp.stack([chip, core, sub, mate, far]).astype(jnp.int32)
+    pair = jnp.concatenate([jnp.stack([keys, values]), jnp.stack([other_keys, other_values])], axis=1)
+    pair, ids = tie((pair, ids))
     near = lax.ppermute(pair, "seq", route(0, 1))
     away = lax.ppermute(pair, "seq", route(1, 1))
-    near, infos, starts = tie((near, infos, starts))
+    *infos, starts = tables(ids, doc_lengths, blk, subs)
+    q_send, d_send, pair_send, infos, starts = tie((queries, dout, pair, infos, starts))
+    q_mate, d_mate = swap_mate(q_send), swap_mate(d_send)
+    pair_far = swap_far(pair_send)
     near_far = swap_far(near)
     away, q_mate, d_mate, pair_far, near_far = tie((away, q_mate, d_mate, pair_far, near_far))
     most = jnp.concatenate([near, away, near_far], axis=1)
@@ -426,23 +446,26 @@
     theirs = swap_mate(theirs)
     grad_a = (grad_a.astype(f32) + swap_core(grad_b).astype(f32)).astype(bf16)
     grad_a, dq = tie((grad_a, dq))
-    grad_far = swap_far(grad_a)
+    grad_far = swap_far(grad_a[:, : HALF * blk])
+    far_own = grad_a[:, HALF * blk :]
     grad_a, grad_b, dq = backward(infos[0], *common, (most, most_x), near_pieces[:2], "half", (dq,))
     grad_b, grad_far, theirs = tie((grad_b, grad_far, theirs))
-    home = (grad_a.astype(f32) + swap_core(grad_b).astype(f32) + grad_far[:, : HALF * blk].astype(f32)).astype(bf16)
+    home = (grad_a.astype(f32) + swap_core(grad_b).astype(f32) + grad_far.astype(f32)).astype(bf16)
     home, dq = tie((home, dq))
     near = lax.ppermute(home[:, : 2 * blk], "seq", route(0, -1))
     away = lax.ppermute(home[:, 2 * blk :], "seq", route(1, -1))
-    grad_own, grad_other, attended, dq_mine, dq_mate = backward(
-        infos[0], *common, (pair,), ((0, 0, 2),), "own", (dq, mine, theirs)
-    )
-    dq_back = swap_mate(dq_mate)
-    near, away, grad_own, grad_other = tie((near, away, grad_own, grad_other))
+    grad_own, grad_other, dq, dq_send = backward(infos[0], *common, (pair,), ((0, 0, 2),), "own", (dq,))
+    dq_send, far_own = tie((dq_send, far_own))
+    dq_back = swap_mate(dq_send)
+    grad_far_own = swap_far(far_own)
+    near, away, grad_own, grad_other, theirs = tie((near, away, grad_own, grad_other, theirs))
+    attended = finish(output_kernel, "output", stats, common[-1], mine, theirs)
     back = near.astype(f32) + away.astype(f32)
     other = swap_core((back[:, blk:] + grad_other.astype(f32)).astype(bf16))
-    query_grad = (dq_mine + dq_back.astype(f32)).astype(bf16)
+    dq_back, attended = tie((dq_back, attended))
+    query_grad = finish(query_grad_kernel, "query_grad", dq, dq_back)
     total = [
-        (grad_own[i].astype(f32) + grad_far[i, HALF * blk :].astype(f32) + back[i, :blk] + other[i].astype(f32)).astype(bf16)
+        (grad_own[i].astype(f32) + grad_far_own[i].astype(f32) + back[i, :blk] + other[i].astype(f32)).astype(bf16)
         for i in range(2)
     ]
     return attended, query_grad, total[0], total[1]

time: 108 us -> 113 us (1.046)
  Pallas kernels: 14 us -> 53.4 us
  starting transfers between devices: 45.2 us -> 25 us
  waiting for transfers between devices: 44 us -> 27.5 us
  local copies, waits for them, and re-layouts: 0.82 us -> 3.16 us
    pallas_call x3, Pallas kernels: 8.41 us -> 30.1 us  [backward(): pl.pallas_call(functools.partial(backward_kernel, heads, hd, span, pieces...]
    pallas_call x2, Pallas kernels: 4.04 us -> 17.7 us  [forward(): pl.pallas_call(functools.partial(forward_kernel, heads, hd, share, pieces...]
    ppermute x1, starting transfers between devices: 12.3 us -> 1.92 us  [per_device(): away = lax.ppermute(home[:, 2 * blk:], 'seq', route(1, -1))]
    ppermute x1, starting transfers between devices: 12.1 us -> 1.92 us  [per_device(): near = lax.ppermute(home[:, :2 * blk], 'seq', route(0, -1))]
    ppermute x4 -> x5, waiting for transfers between devices: 15.2 us -> 5.58 us  [swap_far(): lax.ppermute(value, 'sub', [(s, (s + 2 * (s % 2) - 1) % subs) for s in ra...]
    ppermute x5, waiting for transfers between devices: 15.9 us -> 11.3 us  [swap_mate(): return lax.ppermute(value, 'sub', [(s, s ^ 1) for s in range(subs)])]
    ppermute x1, waiting for transfers between devices: 4.57 us -> 0.01 us  [per_device(): away = lax.ppermute(pair, 'seq', route(1, 1))]
    pallas_call x0 -> x2, Pallas kernels: none -> 3.99 us  [finish(): pl.pallas_call(functools.partial(kernel, heads, hd), out_shape=jax.ShapeD...]
  transfers between devices with their start and end apart: 20 -> 21, of which waited for: 15 -> 13; matrix products, arithmetic and copies ran while one was open for 1% -> 1% of each run, Pallas kernels for 8% -> 27%
where the time goes in v1:
time: 113 us; the launch traced here: 112 us
  Pallas kernels  53.4 us (47%)
  waiting for transfers between devices  27.5 us (24%)
  starting transfers between devices  25 us (22%)
  local copies, waits for them, and re-layouts  3.16 us (3%)
  other arithmetic  2.12 us (2%)
    pallas_call x3, Pallas kernels, backward(): pl.pallas_call(functools.partial(backward_kernel, heads, hd, span, pieces...  30.1 us
    pallas_call x2, Pallas kernels, forward(): pl.pallas_call(functools.partial(forward_kernel, heads, hd, share, pieces...  17.7 us
    ppermute x5, waiting for transfers between devices, swap_mate(): return lax.ppermute(value, 'sub', [(s, s ^ 1) for s in range(subs)])  11.3 us
    ppermute x5, starting transfers between devices, swap_far(): lax.ppermute(value, 'sub', [(s, (s + 2 * (s % 2) - 1) % subs) for s in ra...  8.57 us
    ppermute x7, waiting for transfers between devices, swap_core(): return lax.ppermute(value, 'seq', [(s, s ^ 1) for s in range(seqs)])  5.98 us
    ppermute x5, waiting for transfers between devices, swap_far(): lax.ppermute(value, 'sub', [(s, (s + 2 * (s % 2) - 1) % subs) for s in ra...  5.58 us
    ppermute x1, starting transfers between devices, per_device(): away = lax.ppermute(pair, 'seq', route(1, 1))  4.81 us
    pallas_call x2, Pallas kernels, finish(): pl.pallas_call(functools.partial(kernel, heads, hd), out_shape=jax.ShapeD...  3.99 us
  transfers between devices with their start and end apart: 21, of which 13 were waited for; matrix products, arithmetic and copies ran while one was open for 1% of the time, Pallas kernels for 27%

profile of v1, /device:TPU:4, one launch (start us, length us, event | category | flops | bytes accessed | tf_op | source)
XLA Modules:
  0.0 112.2 jit_solution(7084001793880176138)
XLA Ops:
  0.6 0.1 collective-permute-start
  0.7 0.5 collective-permute-start.1
  1.2 0.7 stack.47.ids_ref
  1.9 0.3 collective-permute-done
  2.2 0.2 collective-permute-done.1
  2.3 0.9 maximum_maximum_fusion.rest_2_.rest_0_
  3.3 3.5 %collective-permute-start.6 = (bf16[2,512,128]{2,1,0:T(8,128)(2,1)S(1)}, bf16[2,512,128]{2,1,0:T(8,128)(2,1)S(1)}, u32[]{:S(2)}, u32[]{:S(2)}) collective-permute-start(bf16[2,512,128]{2,1,0:T(8,128)(2,1)S(1)} %maximum_maximum_fusion.rest_2_.rest_0_), channel_id=1, source_target_pairs={{0,8},{4,28},{8,16},{12,36},{16,24},{20,44},{24,32},{28,52},{32,40... | collective-permute-start | bytes 786440 | tf_op jit(solution)/shard_map/ppermute | solution.py:425
  6.8 4.8 %collective-permute-start.2 = (bf16[2,512,128]{2,1,0:T(8,128)(2,1)S(1)}, bf16[2,512,128]{2,1,0:T(8,128)(2,1)S(1)}, u32[]{:S(2)}, u32[]{:S(2)}) collective-permute-start(bf16[2,512,128]{2,1,0:T(8,128)(2,1)S(1)} %maximum_maximum_fusion.rest_2_.rest_0_), channel_id=1, source_target_pairs={{0,16},{4,36},{8,24},{12,44},{16,32},{20,52},{24,40},{28,60},{32,4... | collective-permute-start | bytes 786440 | tf_op jit(solution)/shard_map/ppermute | solution.py:426
  11.6 1.6 %tile_tables.1 = (s32[36]{0:T(128)}, s32[36]{0:T(128)}, s32[2,1,256]{2,1,0:T(1,128)}) custom-call(s32[5]{0:T(128)} %stack.47.ids_ref, s32[32]{0:T(128)} %len_ref.1), custom_call_target="tpu_custom_call" | custom-call | tf_op jit(solution)/shard_map/tile_tables/pallas_call | solution.py:70
  13.2 2.0 %collective-permute-start.3 = (bf16[256,512]{1,0:T(8,128)(2,1)}, bf16[256,512]{1,0:T(8,128)(2,1)S(1)}, u32[]{:S(2)}, u32[]{:S(2)}) collective-permute-start(bf16[256,512]{1,0:T(8,128)(2,1)} %q0_ref.9), channel_id=1, source_target_pairs={{0,1},{1,0},{2,3},{3,2},{4,5},{5,4},{6,7},{7,6},{8,9},{9,8},{10,11... | collective-permute-start | bytes 786440 | tf_op jit(solution)/shard_map/ppermute | solution.py:411
  15.2 0.1 collective-permute-start.4
  15.3 4.0 %collective-permute-start.5 = (bf16[2,512,128]{2,1,0:T(8,128)(2,1)S(1)}, bf16[2,512,128]{2,1,0:T(8,128)(2,1)S(1)}, u32[]{:S(2)}, u32[]{:S(2)}) collective-permute-start(bf16[2,512,128]{2,1,0:T(8,128)(2,1)S(1)} %maximum_maximum_fusion.rest_2_.rest_0_), channel_id=1, source_target_pairs={{0,3},{1,2},{2,1},{3,0},{4,7},{5,6},{6,5},{7,4},{8,11},{9,10},{10,... | collective-permute-start | bytes 786440 | tf_op jit(solution)/shard_map/ppermute | solution.py:414
  19.4 1.1 %collective-permute-start.7 = (bf16[2,512,128]{2,1,0:T(8,128)(2,1)S(1)}, bf16[2,512,128]{2,1,0:T(8,128)(2,1)S(1)}, u32[]{:S(2)}, u32[]{:S(2)}) collective-permute-start(bf16[2,512,128]{2,1,0:T(8,128)(2,1)S(1)} %collective-permute-done.6), channel_id=1, source_target_pairs={{0,3},{1,2},{2,1},{3,0},{4,7},{5,6},{6,5},{7,4},{8,11},{9,10},{10,... | collective-permute-start | bytes 786440 | tf_op jit(solution)/shard_map/ppermute | solution.py:414
  20.5 2.2 %collective-permute-done.3.q1_ref = bf16[256,512]{1,0:T(8,128)(2,1)S(1)} collective-permute-done((bf16[256,512]{1,0:T(8,128)(2,1)}, bf16[256,512]{1,0:T(8,128)(2,1)S(1)}, u32[]{:S(2)}, u32[]{:S(2)}) %collective-permute-start.3) | collective-permute-done | bytes 262176 | tf_op jit(solution)/shard_map/ppermute | solution.py:411
  22.7 4.3 %collective-permute-done.4.rest_9_.d1_ref = bf16[256,512]{1,0:T(8,128)(2,1)S(1)} collective-permute-done((bf16[256,512]{1,0:T(8,128)(2,1)}, bf16[256,512]{1,0:T(8,128)(2,1)S(1)}, u32[]{:S(2)}, u32[]{:S(2)}) %collective-permute-start.4) | collective-permute-done | bytes 262176 | tf_op jit(solution)/shard_map/ppermute | solution.py:411
  27.1 3.4 %collective-permute-done.7 = bf16[2,512,128]{2,1,0:T(8,128)(2,1)S(1)} collective-permute-done((bf16[2,512,128]{2,1,0:T(8,128)(2,1)S(1)}, bf16[2,512,128]{2,1,0:T(8,128)(2,1)S(1)}, u32[]{:S(2)}, u32[]{:S(2)}) %collective-permute-start.7) | collective-permute-done | bytes 262176 | tf_op jit(solution)/shard_map/ppermute | solution.py:414
  30.5 0.1 collective-permute-start.8
  30.6 3.0 %collective-permute-start.9 = (bf16[2,512,128]{2,1,0:T(8,128)(2,1)S(1)}, bf16[2,512,128]{2,1,0:T(8,128)(2,1)S(1)}, u32[]{:S(2)}, u32[]{:S(2)}) collective-permute-start(bf16[2,512,128]{2,1,0:T(8,128)(2,1)S(1)} %collective-permute-done.2), channel_id=1, source_target_pairs={{0,3},{1,2},{2,1},{3,0},{4,7},{5,6},{6,5},{7,4},{8,11},{9,10},{10,... | collective-permute-start | bytes 786440 | tf_op jit(solution)/shard_map/ppermute | solution.py:414
  33.7 8.7 %forward_part.2 = (f32[8,1,256]{2,1,0:T(1,128)S(1)}, f32[8,1,256]{2,1,0:T(1,128)S(1)}, f32[8,128,256]{2,1,0:T(8,128)S(1)}) custom-call(s32[36]{0:T(128)S(1)} %copy-done.7, s32[2,1,256]{2,1,0:T(1,128)S(1)} %copy-done.6, bf16[256,512]{1,0:T(8,128)(2,1)S(1)} %copy-done.4, bf16[256,512]{1,0:T(8,128)(2,1)S(1)} %collective-permute-done.3.q1_ref, ...), custom_call_target="tpu_custom_call" | custom-call | flops 2684354560 | bytes 4194304 | tf_op jit(solution)/shard_map/forward_part/pallas_call | solution.py:223
  42.4 0.1 collective-permute-start.10
  42.5 1.5 %collective-permute-done.10.rest_3_ = bf16[2,512,128]{2,1,0:T(8,128)(2,1)S(1)} collective-permute-done((bf16[2,512,128]{2,1,0:T(8,128)(2,1)S(1)}, bf16[2,512,128]{2,1,0:T(8,128)(2,1)S(1)}, u32[]{:S(2)}, u32[]{:S(2)}) %collective-permute-start.10) | collective-permute-done | bytes 262176 | tf_op jit(solution)/shard_map/ppermute | solution.py:408
  44.0 8.9 %forward_part.3 = (f32[8,3,256]{2,1,0:T(4,128)S(1)}, f32[4,128,256]{2,1,0:T(8,128)S(1)}, bf16[4,128,256]{2,1,0:T(8,128)(2,1)S(1)}) custom-call(s32[36]{0:T(128)S(1)} %copy-done.8, s32[2,1,256]{2,1,0:T(1,128)S(1)} %copy-done.6, bf16[256,512]{1,0:T(8,128)(2,1)S(1)} %copy-done.4, bf16[256,512]{1,0:T(8,128)(2,1)S(1)} %collective-permute-done.3.q1_ref, ...), custom_call_target="tpu_custom_call" | custom-call | flops 2684354560 | bytes 4194304 | tf_op jit(solution)/shard_map/forward_part/pallas_call | solution.py:223
  53.0 0.8 copy-done
  53.8 3.9 %collective-permute-done.11.sb_ref = f32[8,3,256]{2,1,0:T(4,128)S(1)} collective-permute-done((f32[8,3,256]{2,1,0:T(4,128)S(1)}, f32[8,3,256]{2,1,0:T(4,128)S(1)}, u32[]{:S(2)}, u32[]{:S(2)}) %collective-permute-start.11) | collective-permute-done | bytes 24608 | tf_op jit(solution)/shard_map/ppermute | solution.py:411
  57.7 14.5 %backward_part.3 = (bf16[2,1280,128]{2,1,0:T(8,128)(2,1)S(1)}, bf16[2,1280,128]{2,1,0:T(8,128)(2,1)S(1)}, f32[8,128,256]{2,1,0:T(8,128)S(1)}) custom-call(s32[36]{0:T(128)S(1)} %copy-done.8, s32[2,1,256]{2,1,0:T(1,128)S(1)} %copy-done.6, bf16[256,512]{1,0:T(8,128)(2,1)S(1)} %copy-done.4, bf16[256,512]{1,0:T(8,128)(2,1)S(1)} %collective-permute-done.3.q1_ref, ...), custom_call_target="tpu_custom_call" | custom-call | flops 6710886400 | bytes 4194304 | tf_op jit(solution)/shard_map/backward_part/pallas_call | solution.py:362
  72.2 0.1 collective-permute-start.12
  72.3 2.1 %collective-permute-done.12 = bf16[2,1280,128]{2,1,0:T(8,128)(2,1)S(1)} collective-permute-done((bf16[2,1280,128]{2,1,0:T(8,128)(2,1)S(1)}, bf16[2,1280,128]{2,1,0:T(8,128)(2,1)S(1)}, u32[]{:S(2)}, u32[]{:S(2)}) %collective-permute-start.12) | collective-permute-done | bytes 655392 | tf_op jit(solution)/shard_map/ppermute | solution.py:408
  74.4 0.2 add_convert_fusion
  74.6 0.1 collective-permute-start.13
  74.7 0.1 collective-permute-start.14
  74.8 12.8 %backward_part.4 = (bf16[2,1024,128]{2,1,0:T(8,128)(2,1)S(1)}, bf16[2,1024,128]{2,1,0:T(8,128)(2,1)S(1)}, f32[8,128,256]{2,1,0:T(8,128)S(1)}) custom-call(s32[36]{0:T(128)S(1)} %copy-done.7, s32[2,1,256]{2,1,0:T(1,128)S(1)} %copy-done.6, bf16[256,512]{1,0:T(8,128)(2,1)S(1)} %copy-done.4, bf16[256,512]{1,0:T(8,128)(2,1)S(1)} %collective-permute-done.3.q1_ref, ...), custom_call_target="tpu_custom_call" | custom-call | flops 5368709120 | bytes 4194304 | tf_op jit(solution)/shard_map/backward_part/pallas_call | solution.py:362
  87.7 2.2 %collective-permute-done.13 = bf16[2,1024,128]{2,1,0:T(8,128)(2,1)S(1)} collective-permute-done((bf16[2,1024,128]{2,1,0:T(8,128)(2,1)S(1)}, bf16[2,1024,128]{2,1,0:T(8,128)(2,1)S(1)}, u32[]{:S(2)}, u32[]{:S(2)}) %collective-permute-start.13) | collective-permute-done | bytes 524320 | tf_op jit(solution)/shard_map/ppermute | solution.py:414
  89.9 1.9 %collective-permute-done.15 = bf16[2,1024,128]{2,1,0:T(8,128)(2,1)S(1)} collective-permute-done((bf16[2,1024,128]{2,1,0:T(8,128)(2,1)S(1)}, bf16[2,1024,128]{2,1,0:T(8,128)(2,1)S(1)}, u32[]{:S(2)}, u32[]{:S(2)}) %collective-permute-start.15) | collective-permute-done | bytes 524320 | tf_op jit(solution)/shard_map/ppermute | solution.py:408
  91.8 0.2 add_convert_fusion.1
  92.1 1.9 %collective-permute-start.18 = (bf16[2,512,128]{2,1,0:T(8,128)(2,1)S(1)}, bf16[2,512,128]{2,1,0:T(8,128)(2,1)S(1)}, u32[]{:S(2)}, u32[]{:S(2)}) collective-permute-start(bf16[2,512,128]{2,1,0:T(8,128)(2,1)S(1)} %get-tuple-element.114), channel_id=1, source_target_pairs={{16,0},{36,4},{24,8},{44,12},{32,16},{52,20},{40,24},{60,28},{48,3... | collective-permute-start | bytes 786440 | tf_op jit(solution)/shard_map/ppermute | solution.py:456
  94.0 1.9 %collective-permute-start.17 = (bf16[2,512,128]{2,1,0:T(8,128)(2,1)S(1)}, bf16[2,512,128]{2,1,0:T(8,128)(2,1)S(1)}, u32[]{:S(2)}, u32[]{:S(2)}) collective-permute-start(bf16[2,512,128]{2,1,0:T(8,128)(2,1)S(1)} %get-tuple-element.115), channel_id=1, source_target_pairs={{8,0},{28,4},{16,8},{36,12},{24,16},{44,20},{32,24},{52,28},{40,32... | collective-permute-start | bytes 786440 | tf_op jit(solution)/shard_map/ppermute | solution.py:455
  96.0 2.8 %backward_part.5 = (bf16[2,256,128]{2,1,0:T(8,128)(2,1)S(1)}, bf16[2,256,128]{2,1,0:T(8,128)(2,1)S(1)}, f32[4,128,256]{2,1,0:T(8,128)S(1)}, bf16[4,128,256]{2,1,0:T(8,128)(2,1)S(1)}) custom-call(s32[36]{0:T(128)S(1)} %copy-done.7, s32[2,1,256]{2,1,0:T(1,128)S(1)} %copy-done.6, bf16[256,512]{1,0:T(8,128)(2,1)S(1)} %copy-done.4, ...), custom_call_target="tpu_custom_call" | custom-call | flops 1342177280 | bytes 4194304 | tf_op jit(solution)/shard_map/backward_part/pallas_call | solution.py:362
  98.8 0.8 copy-done.1
  99.6 0.3 collective-permute-start.19
  99.9 1.2 %collective-permute-start.16 = (bf16[4,128,256]{2,1,0:T(8,128)(2,1)S(1)}, bf16[4,128,256]{2,1,0:T(8,128)(2,1)S(1)}, u32[]{:S(2)}, u32[]{:S(2)}) collective-permute-start(bf16[4,128,256]{2,1,0:T(8,128)(2,1)S(1)} %get-tuple-element.97), channel_id=1, source_target_pairs={{0,1},{1,0},{2,3},{3,2},{4,5},{5,4},{6,7},{7,6},{8,9},{9,8},{10,11... | collective-permute-start | bytes 786440 | tf_op jit(solution)/shard_map/ppermute | solution.py:411
  101.1 0.9 collective-permute-done.18
  102.0 3.8 %collective-permute-done.17 = bf16[2,512,128]{2,1,0:T(8,128)(2,1)S(1)} collective-permute-done((bf16[2,512,128]{2,1,0:T(8,128)(2,1)S(1)}, bf16[2,512,128]{2,1,0:T(8,128)(2,1)S(1)}, u32[]{:S(2)}, u32[]{:S(2)}) %collective-permute-start.17) | collective-permute-done | bytes 262176 | tf_op jit(solution)/shard_map/ppermute | solution.py:455
  105.8 0.1 collective-permute-start.20
  105.9 2.0 %output.1 = bf16[256,512]{1,0:T(8,128)(2,1)} custom-call(f32[8,3,256]{2,1,0:T(4,128)} %copy-done.2, f32[8,3,256]{2,1,0:T(4,128)} %copy-done.3, f32[4,128,256]{2,1,0:T(8,128)} %copy-done, bf16[4,128,256]{2,1,0:T(8,128)(2,1)} %copy-done.9), custom_call_target="tpu_custom_call" | custom-call | tf_op jit(solution)/shard_map/output/pallas_call | solution.py:390
  108.0 0.8 collective-permute-done.16.theirs_ref
  108.8 0.7 copy-done.10
  109.5 1.9 %query_grad.1 = bf16[256,512]{1,0:T(8,128)(2,1)} custom-call(f32[4,128,256]{2,1,0:T(8,128)} %copy-done.1, bf16[4,128,256]{2,1,0:T(8,128)(2,1)} %copy-done.10), custom_call_target="tpu_custom_call" | custom-call | tf_op jit(solution)/shard_map/query_grad/pallas_call | solution.py:390
  111.5 0.7 fusion.6
  (37 shorter events, 0.3 us)
Async XLA Ops:
  0.6 1.5 %collective-permute-start = (bf16[256,128]{1,0:T(8,128)(2,1)}, bf16[256,128]{1,0:T(8,128)(2,1)S(1)}, u32[]{:S(2)}, u32[]{:S(2)}) collective-permute-start(bf16[256,128]{1,0:T(8,128)(2,1)} %param.6), channel_id=1, source_target_pairs={{0,4},{4,0},{8,12},{12,8},{16,20},{20,16},{24,28},{28,24},{32,36},... | collective-permute-start | bytes 196616 | tf_op jit(solution)/shard_map/ppermute | solution.py:408
  0.7 1.6 %collective-permute-start.1 = (bf16[256,128]{1,0:T(8,128)(2,1)}, bf16[256,128]{1,0:T(8,128)(2,1)S(1)}, u32[]{:S(2)}, u32[]{:S(2)}) collective-permute-start(bf16[256,128]{1,0:T(8,128)(2,1)} %param.7), channel_id=1, source_target_pairs={{0,4},{4,0},{8,12},{12,8},{16,20},{20,16},{24,28},{28,24},{32,36},... | collective-permute-start | bytes 196616 | tf_op jit(solution)/shard_map/ppermute | solution.py:408
  2.3 31.3 %copy-start.4 = (bf16[256,512]{1,0:T(8,128)(2,1)S(1)}, bf16[256,512]{1,0:T(8,128)(2,1)}, u32[]{:S(2)}) copy-start(bf16[256,512]{1,0:T(8,128)(2,1)} %q0_ref.9) | copy-start | bytes 786436
  3.3 16.1 %collective-permute-start.6 = (bf16[2,512,128]{2,1,0:T(8,128)(2,1)S(1)}, bf16[2,512,128]{2,1,0:T(8,128)(2,1)S(1)}, u32[]{:S(2)}, u32[]{:S(2)}) collective-permute-start(bf16[2,512,128]{2,1,0:T(8,128)(2,1)S(1)} %maximum_maximum_fusion.rest_2_.rest_0_), channel_id=1, source_target_pairs={{0,8},{4,28},{8,16},{12,36},{16,24},{20,44},{24,32},{28,52},{32,40... | collective-permute-start | bytes 786440 | tf_op jit(solution)/shard_map/ppermute | solution.py:425
  6.8 20.3 %collective-permute-start.2 = (bf16[2,512,128]{2,1,0:T(8,128)(2,1)S(1)}, bf16[2,512,128]{2,1,0:T(8,128)(2,1)S(1)}, u32[]{:S(2)}, u32[]{:S(2)}) collective-permute-start(bf16[2,512,128]{2,1,0:T(8,128)(2,1)S(1)} %maximum_maximum_fusion.rest_2_.rest_0_), channel_id=1, source_target_pairs={{0,16},{4,36},{8,24},{12,44},{16,32},{20,52},{24,40},{28,60},{32,4... | collective-permute-start | bytes 786440 | tf_op jit(solution)/shard_map/ppermute | solution.py:426
  13.2 20.5 %copy-start.6 = (s32[2,1,256]{2,1,0:T(1,128)S(1)}, s32[2,1,256]{2,1,0:T(1,128)}, u32[]{:S(2)}) copy-start(s32[2,1,256]{2,1,0:T(1,128)} %get-tuple-element.64.start_ref) | copy-start | bytes 6148
  13.2 20.5 %copy-start.7 = (s32[36]{0:T(128)S(1)}, s32[36]{0:T(128)}, u32[]{:S(2)}) copy-start(s32[36]{0:T(128)} %get-tuple-element.63.info_ref) | copy-start | bytes 436
  13.2 9.5 %collective-permute-start.3 = (bf16[256,512]{1,0:T(8,128)(2,1)}, bf16[256,512]{1,0:T(8,128)(2,1)S(1)}, u32[]{:S(2)}, u32[]{:S(2)}) collective-permute-start(bf16[256,512]{1,0:T(8,128)(2,1)} %q0_ref.9), channel_id=1, source_target_pairs={{0,1},{1,0},{2,3},{3,2},{4,5},{5,4},{6,7},{7,6},{8,9},{9,8},{10,11... | collective-permute-start | bytes 786440 | tf_op jit(solution)/shard_map/ppermute | solution.py:411
  15.2 11.8 %collective-permute-start.4 = (bf16[256,512]{1,0:T(8,128)(2,1)}, bf16[256,512]{1,0:T(8,128)(2,1)S(1)}, u32[]{:S(2)}, u32[]{:S(2)}) collective-permute-start(bf16[256,512]{1,0:T(8,128)(2,1)} %d0_ref.5), channel_id=1, source_target_pairs={{0,1},{1,0},{2,3},{3,2},{4,5},{5,4},{6,7},{7,6},{8,9},{9,8},{10,11... | collective-permute-start | bytes 786440 | tf_op jit(solution)/shard_map/ppermute | solution.py:411
  15.3 11.7 %collective-permute-start.5 = (bf16[2,512,128]{2,1,0:T(8,128)(2,1)S(1)}, bf16[2,512,128]{2,1,0:T(8,128)(2,1)S(1)}, u32[]{:S(2)}, u32[]{:S(2)}) collective-permute-start(bf16[2,512,128]{2,1,0:T(8,128)(2,1)S(1)} %maximum_maximum_fusion.rest_2_.rest_0_), channel_id=1, source_target_pairs={{0,3},{1,2},{2,1},{3,0},{4,7},{5,6},{6,5},{7,4},{8,11},{9,10},{10,... | collective-permute-start | bytes 786440 | tf_op jit(solution)/shard_map/ppermute | solution.py:414
  19.4 11.0 %collective-permute-start.7 = (bf16[2,512,128]{2,1,0:T(8,128)(2,1)S(1)}, bf16[2,512,128]{2,1,0:T(8,128)(2,1)S(1)}, u32[]{:S(2)}, u32[]{:S(2)}) collective-permute-start(bf16[2,512,128]{2,1,0:T(8,128)(2,1)S(1)} %collective-permute-done.6), channel_id=1, source_target_pairs={{0,3},{1,2},{2,1},{3,0},{4,7},{5,6},{6,5},{7,4},{8,11},{9,10},{10,... | collective-permute-start | bytes 786440 | tf_op jit(solution)/shard_map/ppermute | solution.py:414
  30.5 13.5 %copy-start.5 = (bf16[256,512]{1,0:T(8,128)(2,1)S(1)}, bf16[256,512]{1,0:T(8,128)(2,1)}, u32[]{:S(2)}) copy-start(bf16[256,512]{1,0:T(8,128)(2,1)} %d0_ref.5) | copy-start | bytes 786436
  30.5 13.5 %copy-start.8 = (s32[36]{0:T(128)S(1)}, s32[36]{0:T(128)}, u32[]{:S(2)}) copy-start(s32[36]{0:T(128)} %get-tuple-element.70.info_ref) | copy-start | bytes 436
  30.5 3.1 %collective-permute-start.8 = (bf16[2,1536,128]{2,1,0:T(8,128)(2,1)S(1)}, bf16[2,1536,128]{2,1,0:T(8,128)(2,1)S(1)}, u32[]{:S(2)}, u32[]{:S(2)}) collective-permute-start(bf16[2,1536,128]{2,1,0:T(8,128)(2,1)S(1)} %constant_dynamic-update-slice_fusion.rest_0_), channel_id=1, source_target_pairs={{0,4},{4,0},{8,12},{12,8},{16,20},{20,16},{24,28},{28,24},{32,36},... | collective-permute-start | bytes 2359304 | tf_op jit(solution)/shard_map/ppermute | solution.py:408
  30.6 11.8 %collective-permute-start.9 = (bf16[2,512,128]{2,1,0:T(8,128)(2,1)S(1)}, bf16[2,512,128]{2,1,0:T(8,128)(2,1)S(1)}, u32[]{:S(2)}, u32[]{:S(2)}) collective-permute-start(bf16[2,512,128]{2,1,0:T(8,128)(2,1)S(1)} %collective-permute-done.2), channel_id=1, source_target_pairs={{0,3},{1,2},{2,1},{3,0},{4,7},{5,6},{6,5},{7,4},{8,11},{9,10},{10,... | collective-permute-start | bytes 786440 | tf_op jit(solution)/shard_map/ppermute | solution.py:414
  42.4 1.6 %collective-permute-start.10 = (bf16[2,512,128]{2,1,0:T(8,128)(2,1)S(1)}, bf16[2,512,128]{2,1,0:T(8,128)(2,1)S(1)}, u32[]{:S(2)}, u32[]{:S(2)}) collective-permute-start(bf16[2,512,128]{2,1,0:T(8,128)(2,1)S(1)} %collective-permute-done.9.rest_2_), channel_id=1, source_target_pairs={{0,4},{4,0},{8,12},{12,8},{16,20},{20,16},{24,28},{28,24},{32,36},... | collective-permute-start | bytes 786440 | tf_op jit(solution)/shard_map/ppermute | solution.py:408
  53.0 0.8 copy-start
  53.8 42.1 %copy-start.2 = (f32[8,3,256]{2,1,0:T(4,128)}, f32[8,3,256]{2,1,0:T(4,128)S(1)}, u32[]{:S(2)}) copy-start(f32[8,3,256]{2,1,0:T(4,128)S(1)} %get-tuple-element.81.sa_ref) | copy-start | bytes 73732
  53.8 3.9 %collective-permute-start.11 = (f32[8,3,256]{2,1,0:T(4,128)S(1)}, f32[8,3,256]{2,1,0:T(4,128)S(1)}, u32[]{:S(2)}, u32[]{:S(2)}) collective-permute-start(f32[8,3,256]{2,1,0:T(4,128)S(1)} %get-tuple-element.81.sa_ref), channel_id=1, source_target_pairs={{0,1},{1,0},{2,3},{3,2},{4,5},{5,4},{6,7},{7,6},{8,9},{9,8},{10,11... | collective-permute-start | bytes 73736 | tf_op jit(solution)/shard_map/ppermute | solution.py:411
  57.7 38.2 %copy-start.3 = (f32[8,3,256]{2,1,0:T(4,128)}, f32[8,3,256]{2,1,0:T(4,128)S(1)}, u32[]{:S(2)}) copy-start(f32[8,3,256]{2,1,0:T(4,128)S(1)} %collective-permute-done.11.sb_ref) | copy-start | bytes 73732
  72.2 2.2 %collective-permute-start.12 = (bf16[2,1280,128]{2,1,0:T(8,128)(2,1)S(1)}, bf16[2,1280,128]{2,1,0:T(8,128)(2,1)S(1)}, u32[]{:S(2)}, u32[]{:S(2)}) collective-permute-start(bf16[2,1280,128]{2,1,0:T(8,128)(2,1)S(1)} %get-tuple-element.85), channel_id=1, source_target_pairs={{0,4},{4,0},{8,12},{12,8},{16,20},{20,16},{24,28},{28,24},{32,36},... | collective-permute-start | bytes 1966088 | tf_op jit(solution)/shard_map/ppermute | solution.py:408
  74.6 15.3 %collective-permute-start.13 = (bf16[2,1024,128]{2,1,0:T(8,128)(2,1)S(1)}, bf16[2,1024,128]{2,1,0:T(8,128)(2,1)S(1)}, u32[]{:S(2)}, u32[]{:S(2)}) collective-permute-start(bf16[2,1024,128]{2,1,0:T(8,128)(2,1)S(1)} %slice.39), channel_id=1, source_target_pairs={{0,3},{1,2},{2,1},{3,0},{4,7},{5,6},{6,5},{7,4},{8,11},{9,10},{10,... | collective-permute-start | bytes 1572872 | tf_op jit(solution)/shard_map/ppermute | solution.py:414
  74.7 12.9 %collective-permute-start.14 = (bf16[4,128,256]{2,1,0:T(8,128)(2,1)S(1)}, bf16[4,128,256]{2,1,0:T(8,128)(2,1)S(1)}, u32[]{:S(2)}, u32[]{:S(2)}) collective-permute-start(bf16[4,128,256]{2,1,0:T(8,128)(2,1)S(1)} %get-tuple-element.91), channel_id=1, source_target_pairs={{0,1},{1,0},{2,3},{3,2},{4,5},{5,4},{6,7},{7,6},{8,9},{9,8},{10,11... | collective-permute-start | bytes 786440 | tf_op jit(solution)/shard_map/ppermute | solution.py:411
  87.7 4.3 %copy-start.9 = (bf16[4,128,256]{2,1,0:T(8,128)(2,1)}, bf16[4,128,256]{2,1,0:T(8,128)(2,1)S(1)}, u32[]{:S(2)}) copy-start(bf16[4,128,256]{2,1,0:T(8,128)(2,1)S(1)} %collective-permute-done.14.theirs_ref) | copy-start | bytes 786436
  89.9 1.9 %collective-permute-start.15 = (bf16[2,1024,128]{2,1,0:T(8,128)(2,1)S(1)}, bf16[2,1024,128]{2,1,0:T(8,128)(2,1)S(1)}, u32[]{:S(2)}, u32[]{:S(2)}) collective-permute-start(bf16[2,1024,128]{2,1,0:T(8,128)(2,1)S(1)} %get-tuple-element.92), channel_id=1, source_target_pairs={{0,4},{4,0},{8,12},{12,8},{16,20},{20,16},{24,28},{28,24},{32,36},... | collective-permute-start | bytes 1572872 | tf_op jit(solution)/shard_map/ppermute | solution.py:408
  92.1 9.9 %collective-permute-start.18 = (bf16[2,512,128]{2,1,0:T(8,128)(2,1)S(1)}, bf16[2,512,128]{2,1,0:T(8,128)(2,1)S(1)}, u32[]{:S(2)}, u32[]{:S(2)}) collective-permute-start(bf16[2,512,128]{2,1,0:T(8,128)(2,1)S(1)} %get-tuple-element.114), channel_id=1, source_target_pairs={{16,0},{36,4},{24,8},{44,12},{32,16},{52,20},{40,24},{60,28},{48,3... | collective-permute-start | bytes 786440 | tf_op jit(solution)/shard_map/ppermute | solution.py:456
  94.0 11.7 %collective-permute-start.17 = (bf16[2,512,128]{2,1,0:T(8,128)(2,1)S(1)}, bf16[2,512,128]{2,1,0:T(8,128)(2,1)S(1)}, u32[]{:S(2)}, u32[]{:S(2)}) collective-permute-start(bf16[2,512,128]{2,1,0:T(8,128)(2,1)S(1)} %get-tuple-element.115), channel_id=1, source_target_pairs={{8,0},{28,4},{16,8},{36,12},{24,16},{44,20},{32,24},{52,28},{40,32... | collective-permute-start | bytes 786440 | tf_op jit(solution)/shard_map/ppermute | solution.py:455
  98.8 0.8 copy-start.1
  99.6 11.9 %collective-permute-start.19 = (bf16[2,256,128]{2,1,0:T(8,128)(2,1)S(1)}, bf16[2,256,128]{2,1,0:T(8,128)(2,1)S(1)}, u32[]{:S(2)}, u32[]{:S(2)}) collective-permute-start(bf16[2,256,128]{2,1,0:T(8,128)(2,1)S(1)} %slice.40), channel_id=1, source_target_pairs={{0,3},{1,2},{2,1},{3,0},{4,7},{5,6},{6,5},{7,4},{8,11},{9,10},{10,... | collective-permute-start | bytes 393224 | tf_op jit(solution)/shard_map/ppermute | solution.py:414
  99.9 8.9 %collective-permute-start.16 = (bf16[4,128,256]{2,1,0:T(8,128)(2,1)S(1)}, bf16[4,128,256]{2,1,0:T(8,128)(2,1)S(1)}, u32[]{:S(2)}, u32[]{:S(2)}) collective-permute-start(bf16[4,128,256]{2,1,0:T(8,128)(2,1)S(1)} %get-tuple-element.97), channel_id=1, source_target_pairs={{0,1},{1,0},{2,3},{3,2},{4,5},{5,4},{6,7},{7,6},{8,9},{9,8},{10,11... | collective-permute-start | bytes 786440 | tf_op jit(solution)/shard_map/ppermute | solution.py:411
  105.8 5.6 %collective-permute-start.20 = (bf16[2,256,128]{2,1,0:T(8,128)(2,1)S(1)}, bf16[2,256,128]{2,1,0:T(8,128)(2,1)S(1)}, u32[]{:S(2)}, u32[]{:S(2)}) collective-permute-start(bf16[2,256,128]{2,1,0:T(8,128)(2,1)S(1)} %fusion), channel_id=1, source_target_pairs={{0,4},{4,0},{8,12},{12,8},{16,20},{20,16},{24,28},{28,24},{32,36},... | collective-permute-start | bytes 393224 | tf_op jit(solution)/shard_map/ppermute | solution.py:408
  108.8 0.7 copy-start.10
